TPU v7x, 256 devices: a whole 4x4x8 slice. The times are simulated.
256 devices in a mesh: dp: 4 (over z_hi), seq: 64 (over x, z_lo, y, core).
Axes of the slice: x: 4, y: 4, z: 8 (z_hi: 4, z_lo: 2; z = z_hi * 2 + z_lo), core: 2. Of those that a mesh axis runs over, the one named last changes fastest.
Arguments:
- inputs: bfloat16 [12, 16384, 768], P('dp', 'seq'), may hold values from -6 to 6
- dilated_tap_weight: bfloat16 [3, 768, 384], replicated, may hold values from -0.125 to 0.125
- proj_weight: bfloat16 [384, 768], replicated, may hold values from -0.3125 to 0.3125
- cotangent: bfloat16 [12, 16384, 768], P('dp', 'seq'), may hold values from -6 to 6
Outputs:
- block_out: bfloat16 [12, 16384, 768], P('dp', 'seq')
- input_grad: bfloat16 [12, 16384, 768], P('dp', 'seq')
- conv_grad: float32 [6912, 128], P(('dp', 'seq'))
- proj_grad: float32 [2304, 128], P(('dp', 'seq'))
All inputs are finite; a program needn't handle non-finite values.
Results may differ from a plain program's by a relative error of at most 0.0054.
Values may be sent and summed in bfloat16 or wider, within the bound.
A program may use at most 64 MiB of HBM per device.

v0:
```python
import math

import jax
import jax.numpy as jnp
from jax import lax
from jax.sharding import PartitionSpec as P

DILATION_BINS = 512


def from_behind(block, axis, distance):
    devices = range(lax.axis_size(axis))
    route = [(i - distance, i) for i in devices if i - distance in devices]
    return lax.ppermute(block, axis, route)


def flatten(values):
    return values.reshape(-1, values.shape[-1])


def block_pass(inputs, dilated_tap_weight, proj_weight, cotangent, act_near, grad_near):
    x_f = inputs.astype(jnp.float32)
    act_f, act_back = jax.vjp(jax.nn.gelu, x_f)
    gelu_activation = act_f.astype(jnp.bfloat16)
    lower, upper = act_near(gelu_activation)
    kernel_taps = (flatten(lower), flatten(gelu_activation), flatten(upper))
    pre = jnp.dot(kernel_taps[0], dilated_tap_weight[0], preferred_element_type=jnp.float32)
    pre = pre + jnp.dot(kernel_taps[1], dilated_tap_weight[1], preferred_element_type=jnp.float32)
    pre = pre + jnp.dot(kernel_taps[2], dilated_tap_weight[2], preferred_element_type=jnp.float32)
    mid_f, mid_back = jax.vjp(jax.nn.gelu, pre)
    mid = mid_f.astype(jnp.bfloat16)
    branch = jnp.dot(mid, proj_weight, preferred_element_type=jnp.float32)
    out = (flatten(x_f) + branch).astype(jnp.bfloat16).reshape(inputs.shape)
    grad_rows = flatten(cotangent)
    d_mid = jnp.dot(grad_rows, proj_weight.T, preferred_element_type=jnp.float32)
    preactivation_gradient = mid_back(d_mid)[0].astype(jnp.bfloat16)
    proj_term = jnp.dot(mid.T, grad_rows, preferred_element_type=jnp.float32)
    conv_term = jnp.stack(
        [
            jnp.dot(tap.T, preactivation_gradient, preferred_element_type=jnp.float32)
            for tap in kernel_taps
        ]
    )
    d_pre_win = preactivation_gradient.reshape(inputs.shape[0], inputs.shape[1], -1)
    from_upper, from_lower = grad_near(d_pre_win)
    activation_gradient = jnp.dot(
        flatten(from_upper), dilated_tap_weight[0].T, preferred_element_type=jnp.float32
    )
    activation_gradient = activation_gradient + jnp.dot(
        preactivation_gradient, dilated_tap_weight[1].T, preferred_element_type=jnp.float32
    )
    activation_gradient = activation_gradient + jnp.dot(
        flatten(from_lower), dilated_tap_weight[2].T, preferred_element_type=jnp.float32
    )
    d_x = (
        cotangent.astype(jnp.float32) + act_back(activation_gradient.reshape(inputs.shape))[0]
    ).astype(jnp.bfloat16)
    return (out, d_x, conv_term, proj_term)


def local(inputs, dilated_tap_weight, proj_weight, cotangent):
    device_bin_count = inputs.shape[1]
    seq_count = lax.axis_size("seq")
    receptive_span = DILATION_BINS // device_bin_count
    total_rows = inputs.shape[0] * lax.axis_size("dp") * device_bin_count * seq_count
    factor = 1.0 / math.sqrt(total_rows)

    def act_near(values):
        below = from_behind(values, "seq", receptive_span)
        above = from_behind(values, "seq", -receptive_span)
        return (below, above)

    def grad_near(values):
        above = from_behind(values, "seq", -receptive_span)
        below = from_behind(values, "seq", receptive_span)
        return (above, below)

    block_out, input_grad, conv_term, proj_term = block_pass(
        inputs, dilated_tap_weight, proj_weight, cotangent, act_near, grad_near
    )
    conv_flat = (conv_term * factor).reshape(-1, 128)
    proj_flat = (proj_term * factor).reshape(-1, 128)
    conv_grad, proj_grad = (
        lax.psum_scatter(conv_flat, ("dp", "seq"), scatter_dimension=0, tiled=True),
        lax.psum_scatter(proj_flat, ("dp", "seq"), scatter_dimension=0, tiled=True),
    )
    return (block_out, input_grad, conv_grad, proj_grad)


def solution(mesh):
    return jax.shard_map(
        local,
        mesh=mesh,
        in_specs=(P("dp", "seq", None), P(), P(), P("dp", "seq", None)),
        out_specs=(
            P("dp", "seq", None),
            P("dp", "seq", None),
            P(("dp", "seq"), None),
            P(("dp", "seq"), None),
        ),
        check_vma=False,
    )
```

profile of v0, /device:TPU:1, one launch (start us, length us, event | category | flops | bytes accessed | tf_op | source)
XLA Modules:
  0.0 1188.9 jit_solution(8097867177464805931)
XLA Ops:
  7.2 2.2 fusion.3
  10.8 4.7 collective-permute-start
  17.6 19.3 %collective-permute-done.1 = bf16[3,256,768]{2,1,0:T(8,128)(2,1)S(1)} collective-permute-done((bf16[3,256,768]{2,1,0:T(8,128)(2,1)S(1)}, bf16[3,256,768]{2,1,0:T(8,128)(2,1)S(1)}, u32[]{:S(2)}, u32[]{:S(2)}) %collective-permute-start.1) | collective-permute-done | bytes 1179680 | tf_op jit(solution)/shard_map/ppermute | solution.py:14
  37.8 2.3 fusion.19
  40.2 2.3 convolution_bitcast_fusion
  42.4 1.9 convolution_bitcast_fusion.2
  44.3 1.9 convolution_bitcast_fusion.1
  46.2 2.1 maximum_multiply_fusion
  48.3 4.6 mul.136
  52.8 677.8 %fusion = f32[32,128]{1,0:T(8,128)S(1)} fusion(f32[6912,128]{1,0:T(8,128)} %mul.136), kind=kCustom, calls=%all-reduce-scatter | all-reduce-scatter fusion | flops 1048577 | bytes 3555328
  741.1 13.9 %collective-permute-start.17 = (f32[32,128]{1,0:T(8,128)S(1)}, f32[32,128]{1,0:T(8,128)S(1)}, u32[]{:S(2)}, u32[]{:S(2)}) collective-permute-start(f32[32,128]{1,0:T(8,128)S(1)} %fusion), channel_id=1, source_target_pairs={{0,14},{1,15},{2,16},{3,17},{4,18},{5,19},{6,20},{7,21},{8,22},{9,... | collective-permute-start | bytes 49160
  755.1 14.4 %collective-permute-start.18 = (f32[32,128]{1,0:T(8,128)S(1)}, f32[32,128]{1,0:T(8,128)S(1)}, u32[]{:S(2)}, u32[]{:S(2)}) collective-permute-start(f32[32,128]{1,0:T(8,128)S(1)} %fusion), channel_id=1, source_target_pairs={{0,15},{1,16},{2,17},{3,18},{4,19},{5,20},{6,21},{7,22},{8,23},{9,... | collective-permute-start | bytes 49160
  770.9 2.5 collective-permute-start.20
  773.4 3.4 collective-permute-start.21
  776.8 2.8 collective-permute-start.22
  779.6 3.2 collective-permute-start.23
  782.9 6.0 collective-permute-start.24
  790.2 3.2 collective-permute-start.26
  793.4 2.0 collective-permute-start.27
  795.4 3.4 collective-permute-start.28
  798.9 3.6 collective-permute-start.29
  802.5 2.6 collective-permute-start.30
  805.1 2.2 collective-permute-start.31
  808.7 1.7 collective-permute-start.33
  810.4 3.7 collective-permute-start.34
  814.2 1.6 collective-permute-start.35
  818.4 2.9 collective-permute-start.38
  821.3 2.6 collective-permute-start.39
  823.9 4.7 collective-permute-start.4
  828.6 7.2 collective-permute-start.40
  835.9 2.0 fusion.11
  838.1 5.9 collective-permute-start.41
  844.1 4.9 collective-permute-start.42
  849.0 8.5 collective-permute-start.5
  857.6 13.7 %collective-permute-start.6 = (f32[32,128]{1,0:T(8,128)S(1)}, f32[32,128]{1,0:T(8,128)}, u32[]{:S(2)}, u32[]{:S(2)}) collective-permute-start(f32[32,128]{1,0:T(8,128)S(1)} %fusion), channel_id=1, source_target_pairs={{0,3},{1,4},{2,5},{3,6},{4,7},{5,8},{6,9},{7,10},{8,11},{9,12},{10... | collective-permute-start | bytes 49160
  871.9 1.4 collective-permute-start.2
  873.3 2.0 fusion.26
  875.4 14.4 %collective-permute-start.7 = (f32[32,128]{1,0:T(8,128)S(1)}, f32[32,128]{1,0:T(8,128)}, u32[]{:S(2)}, u32[]{:S(2)}) collective-permute-start(f32[32,128]{1,0:T(8,128)S(1)} %fusion), channel_id=1, source_target_pairs={{0,4},{1,5},{2,6},{3,7},{4,8},{5,9},{6,10},{7,11},{8,12},{9,13},{1... | collective-permute-start | bytes 49160
  889.7 13.1 %collective-permute-start.8 = (f32[32,128]{1,0:T(8,128)S(1)}, f32[32,128]{1,0:T(8,128)}, u32[]{:S(2)}, u32[]{:S(2)}) collective-permute-start(f32[32,128]{1,0:T(8,128)S(1)} %fusion), channel_id=1, source_target_pairs={{0,5},{1,6},{2,7},{3,8},{4,9},{5,10},{6,11},{7,12},{8,13},{9,14},{... | collective-permute-start | bytes 49160
  902.9 13.1 %collective-permute-start.9 = (f32[32,128]{1,0:T(8,128)S(1)}, f32[32,128]{1,0:T(8,128)}, u32[]{:S(2)}, u32[]{:S(2)}) collective-permute-start(f32[32,128]{1,0:T(8,128)S(1)} %fusion), channel_id=1, source_target_pairs={{0,6},{1,7},{2,8},{3,9},{4,10},{5,11},{6,12},{7,13},{8,14},{9,15},... | collective-permute-start | bytes 49160
  916.1 3.5 collective-permute-start.3
  919.6 1.8 convolution_multiply_fusion
  921.4 2.3 reshape.55
  923.8 56.5 %concatenate = f32[1307,128]{1,0:T(8,128)} concatenate(f32[27,128]{1,0:T(8,128)} %copy-done.9, f32[32,128]{1,0:T(8,128)} %copy-done.41, f32[32,128]{1,0:T(8,128)} %copy-done.40, f32[32,128]{1,0:T(8,128)} %copy-done.39, f32[32,128]{1,0:T(8,128)} %copy-done.37, f32[32,128]{1,0:T(8,128)} %copy-done.36, f32[32,128]{1,0:T(8,128)} %copy-done.35, f32[32,128]{1,0:T(8,128)} %copy-done.34, ...), dimensions={0} | concatenate | bytes 1338368
  981.6 2.0 fusion.30
  983.7 2.1 add_add_fusion
  985.8 2.8 fusion.10
  988.7 192.1 %all-reduce.5.cloned.1.call-done = f32[2304,128]{1,0:T(8,128)} async-done(((f32[2304,128]{1,0:T(8,128)}), f32[2304,128]{1,0:T(8,128)}) %all-reduce.5.cloned.1.call-update) | async-done | bytes 1179664
  (155 shorter events, 24.6 us)
Async XLA Ops:
  7.2 1173.6 %all-reduce.5.cloned.1.call-start = ((), (), s32[]{:S(2)}) async-start(), calls=%async_computation | async-start | bytes 2359296
  9.5 27.5 %collective-permute-start.1 = (bf16[3,256,768]{2,1,0:T(8,128)(2,1)S(1)}, bf16[3,256,768]{2,1,0:T(8,128)(2,1)S(1)}, u32[]{:S(2)}, u32[]{:S(2)}) collective-permute-start(bf16[3,256,768]{2,1,0:T(8,128)(2,1)S(1)} %fusion.3), channel_id=1, source_target_pairs={{2,0},{3,1},{4,2},{5,3},{6,4},{7,5},{8,6},{9,7},{10,8},{11,9},{12,... | collective-permute-start | bytes 3538952 | tf_op jit(solution)/shard_map/ppermute | solution.py:14
  10.8 27.1 %collective-permute-start = (bf16[3,256,768]{2,1,0:T(8,128)(2,1)S(1)}, bf16[3,256,768]{2,1,0:T(8,128)(2,1)S(1)}, u32[]{:S(2)}, u32[]{:S(2)}) collective-permute-start(bf16[3,256,768]{2,1,0:T(8,128)(2,1)S(1)} %fusion.3), channel_id=1, source_target_pairs={{0,2},{1,3},{2,4},{3,5},{4,6},{5,7},{6,8},{7,9},{8,10},{9,11},{10,... | collective-permute-start | bytes 3538952 | tf_op jit(solution)/shard_map/ppermute | solution.py:14
  40.2 795.7 %copy-start.43 = (f32[768,384]{1,0:T(8,128)}, f32[768,384]{1,0:T(8,128)S(1)}, u32[]{:S(2)}) copy-start(f32[768,384]{1,0:T(8,128)S(1)} %get-tuple-element.5) | copy-start | bytes 3538948
  52.8 783.1 %copy-start.2 = (bf16[3,256,768]{2,1,0:T(8,128)(2,1)S(1)}, bf16[3,256,768]{2,1,0:T(8,128)(2,1)}, u32[]{:S(2)}) copy-start(bf16[3,256,768]{2,1,0:T(8,128)(2,1)} %param.4) | copy-start | bytes 3538948
  730.6 7.8 collective-permute-start.10
  731.9 7.8 collective-permute-start.11
  733.3 3.9 collective-permute-start.43
  734.6 6.6 collective-permute-start.12
  735.9 19.2 %collective-permute-start.13 = (f32[32,128]{1,0:T(8,128)S(1)}, f32[32,128]{1,0:T(8,128)S(1)}, u32[]{:S(2)}, u32[]{:S(2)}) collective-permute-start(f32[32,128]{1,0:T(8,128)S(1)} %fusion), channel_id=1, source_target_pairs={{0,10},{1,11},{2,12},{3,13},{4,14},{5,15},{6,16},{7,17},{8,18},{9,... | collective-permute-start | bytes 49160
  737.2 100.7 %copy-start.9 = (f32[27,128]{1,0:T(8,128)}, f32[27,128]{1,0:T(8,128)S(1)}, u32[]{:S(2)}) copy-start(f32[27,128]{1,0:T(8,128)S(1)} %collective-permute-done.43) | copy-start | bytes 41476
  737.2 32.3 %collective-permute-start.14 = (f32[32,128]{1,0:T(8,128)S(1)}, f32[32,128]{1,0:T(8,128)S(1)}, u32[]{:S(2)}, u32[]{:S(2)}) collective-permute-start(f32[32,128]{1,0:T(8,128)S(1)} %fusion), channel_id=1, source_target_pairs={{0,11},{1,12},{2,13},{3,14},{4,15},{5,16},{6,17},{7,18},{8,19},{9,... | collective-permute-start | bytes 49160
  738.5 32.4 %collective-permute-start.15 = (f32[32,128]{1,0:T(8,128)S(1)}, f32[32,128]{1,0:T(8,128)S(1)}, u32[]{:S(2)}, u32[]{:S(2)}) collective-permute-start(f32[32,128]{1,0:T(8,128)S(1)} %fusion), channel_id=1, source_target_pairs={{0,12},{1,13},{2,14},{3,15},{4,16},{5,17},{6,18},{7,19},{8,20},{9,... | collective-permute-start | bytes 49160
  739.8 33.6 %collective-permute-start.16 = (f32[32,128]{1,0:T(8,128)S(1)}, f32[32,128]{1,0:T(8,128)S(1)}, u32[]{:S(2)}, u32[]{:S(2)}) collective-permute-start(f32[32,128]{1,0:T(8,128)S(1)} %fusion), channel_id=1, source_target_pairs={{0,13},{1,14},{2,15},{3,16},{4,17},{5,18},{6,19},{7,20},{8,21},{9,... | collective-permute-start | bytes 49160
  741.1 35.7 %collective-permute-start.17 = (f32[32,128]{1,0:T(8,128)S(1)}, f32[32,128]{1,0:T(8,128)S(1)}, u32[]{:S(2)}, u32[]{:S(2)}) collective-permute-start(f32[32,128]{1,0:T(8,128)S(1)} %fusion), channel_id=1, source_target_pairs={{0,14},{1,15},{2,16},{3,17},{4,18},{5,19},{6,20},{7,21},{8,22},{9,... | collective-permute-start | bytes 49160
  755.1 24.5 %collective-permute-start.18 = (f32[32,128]{1,0:T(8,128)S(1)}, f32[32,128]{1,0:T(8,128)S(1)}, u32[]{:S(2)}, u32[]{:S(2)}) collective-permute-start(f32[32,128]{1,0:T(8,128)S(1)} %fusion), channel_id=1, source_target_pairs={{0,15},{1,16},{2,17},{3,18},{4,19},{5,20},{6,21},{7,22},{8,23},{9,... | collective-permute-start | bytes 49160
  769.5 13.3 %collective-permute-start.19 = (f32[32,128]{1,0:T(8,128)S(1)}, f32[32,128]{1,0:T(8,128)S(1)}, u32[]{:S(2)}, u32[]{:S(2)}) collective-permute-start(f32[32,128]{1,0:T(8,128)S(1)} %fusion), channel_id=1, source_target_pairs={{0,16},{1,17},{2,18},{3,19},{4,20},{5,21},{6,22},{7,23},{8,24},{9,... | collective-permute-start | bytes 49160
  770.9 17.9 %collective-permute-start.20 = (f32[32,128]{1,0:T(8,128)S(1)}, f32[32,128]{1,0:T(8,128)S(1)}, u32[]{:S(2)}, u32[]{:S(2)}) collective-permute-start(f32[32,128]{1,0:T(8,128)S(1)} %fusion), channel_id=1, source_target_pairs={{0,17},{1,18},{2,19},{3,20},{4,21},{5,22},{6,23},{7,24},{8,25},{9,... | collective-permute-start | bytes 49160
  773.4 16.7 %collective-permute-start.21 = (f32[32,128]{1,0:T(8,128)S(1)}, f32[32,128]{1,0:T(8,128)S(1)}, u32[]{:S(2)}, u32[]{:S(2)}) collective-permute-start(f32[32,128]{1,0:T(8,128)S(1)} %fusion), channel_id=1, source_target_pairs={{0,18},{1,19},{2,20},{3,21},{4,22},{5,23},{6,24},{7,25},{8,26},{9,... | collective-permute-start | bytes 49160
  776.8 16.6 %collective-permute-start.22 = (f32[32,128]{1,0:T(8,128)S(1)}, f32[32,128]{1,0:T(8,128)S(1)}, u32[]{:S(2)}, u32[]{:S(2)}) collective-permute-start(f32[32,128]{1,0:T(8,128)S(1)} %fusion), channel_id=1, source_target_pairs={{0,19},{1,20},{2,21},{3,22},{4,23},{5,24},{6,25},{7,26},{8,27},{9,... | collective-permute-start | bytes 49160
  779.6 15.7 %collective-permute-start.23 = (f32[32,128]{1,0:T(8,128)S(1)}, f32[32,128]{1,0:T(8,128)S(1)}, u32[]{:S(2)}, u32[]{:S(2)}) collective-permute-start(f32[32,128]{1,0:T(8,128)S(1)} %fusion), channel_id=1, source_target_pairs={{0,20},{1,21},{2,22},{3,23},{4,24},{5,25},{6,26},{7,27},{8,28},{9,... | collective-permute-start | bytes 49160
  782.9 16.0 %collective-permute-start.24 = (f32[32,128]{1,0:T(8,128)S(1)}, f32[32,128]{1,0:T(8,128)S(1)}, u32[]{:S(2)}, u32[]{:S(2)}) collective-permute-start(f32[32,128]{1,0:T(8,128)S(1)} %fusion), channel_id=1, source_target_pairs={{0,21},{1,22},{2,23},{3,24},{4,25},{5,26},{6,27},{7,28},{8,29},{9,... | collective-permute-start | bytes 49160
  788.9 13.6 %collective-permute-start.25 = (f32[32,128]{1,0:T(8,128)S(1)}, f32[32,128]{1,0:T(8,128)S(1)}, u32[]{:S(2)}, u32[]{:S(2)}) collective-permute-start(f32[32,128]{1,0:T(8,128)S(1)} %fusion), channel_id=1, source_target_pairs={{0,22},{1,23},{2,24},{3,25},{4,26},{5,27},{6,28},{7,29},{8,30},{9,... | collective-permute-start | bytes 49160
  790.2 14.9 %collective-permute-start.26 = (f32[32,128]{1,0:T(8,128)S(1)}, f32[32,128]{1,0:T(8,128)S(1)}, u32[]{:S(2)}, u32[]{:S(2)}) collective-permute-start(f32[32,128]{1,0:T(8,128)S(1)} %fusion), channel_id=1, source_target_pairs={{0,23},{1,24},{2,25},{3,26},{4,27},{5,28},{6,29},{7,30},{8,31},{9,... | collective-permute-start | bytes 49160
  793.4 13.9 %collective-permute-start.27 = (f32[32,128]{1,0:T(8,128)S(1)}, f32[32,128]{1,0:T(8,128)S(1)}, u32[]{:S(2)}, u32[]{:S(2)}) collective-permute-start(f32[32,128]{1,0:T(8,128)S(1)} %fusion), channel_id=1, source_target_pairs={{0,24},{1,25},{2,26},{3,27},{4,28},{5,29},{6,30},{7,31},{8,32},{9,... | collective-permute-start | bytes 49160
  795.4 13.3 %collective-permute-start.28 = (f32[32,128]{1,0:T(8,128)S(1)}, f32[32,128]{1,0:T(8,128)S(1)}, u32[]{:S(2)}, u32[]{:S(2)}) collective-permute-start(f32[32,128]{1,0:T(8,128)S(1)} %fusion), channel_id=1, source_target_pairs={{0,25},{1,26},{2,27},{3,28},{4,29},{5,30},{6,31},{7,32},{8,33},{9,... | collective-permute-start | bytes 49160
  798.9 11.6 collective-permute-start.29
  802.5 11.7 collective-permute-start.30
  805.1 10.6 collective-permute-start.31
  807.4 9.7 collective-permute-start.32
  808.7 9.7 collective-permute-start.33
  810.4 10.8 collective-permute-start.34
  814.2 9.7 collective-permute-start.35
  815.8 12.9 %collective-permute-start.36 = (f32[32,128]{1,0:T(8,128)S(1)}, f32[32,128]{1,0:T(8,128)S(1)}, u32[]{:S(2)}, u32[]{:S(2)}) collective-permute-start(f32[32,128]{1,0:T(8,128)S(1)} %fusion), channel_id=1, source_target_pairs={{0,33},{1,34},{2,35},{3,36},{4,37},{5,38},{6,39},{7,40},{8,41},{9,... | collective-permute-start | bytes 49160
  817.1 21.1 %collective-permute-start.37 = (f32[32,128]{1,0:T(8,128)S(1)}, f32[32,128]{1,0:T(8,128)S(1)}, u32[]{:S(2)}, u32[]{:S(2)}) collective-permute-start(f32[32,128]{1,0:T(8,128)S(1)} %fusion), channel_id=1, source_target_pairs={{0,34},{1,35},{2,36},{3,37},{4,38},{5,39},{6,40},{7,41},{8,42},{9,... | collective-permute-start | bytes 49160
  818.4 25.6 %collective-permute-start.38 = (f32[32,128]{1,0:T(8,128)S(1)}, f32[32,128]{1,0:T(8,128)S(1)}, u32[]{:S(2)}, u32[]{:S(2)}) collective-permute-start(f32[32,128]{1,0:T(8,128)S(1)} %fusion), channel_id=1, source_target_pairs={{0,35},{1,36},{2,37},{3,38},{4,39},{5,40},{6,41},{7,42},{8,43},{9,... | collective-permute-start | bytes 49160
  821.3 27.7 %collective-permute-start.39 = (f32[32,128]{1,0:T(8,128)S(1)}, f32[32,128]{1,0:T(8,128)S(1)}, u32[]{:S(2)}, u32[]{:S(2)}) collective-permute-start(f32[32,128]{1,0:T(8,128)S(1)} %fusion), channel_id=1, source_target_pairs={{0,36},{1,37},{2,38},{3,39},{4,40},{5,41},{6,42},{7,43},{8,44},{9,... | collective-permute-start | bytes 49160
  823.9 33.7 %collective-permute-start.4 = (f32[32,128]{1,0:T(8,128)S(1)}, f32[32,128]{1,0:T(8,128)S(1)}, u32[]{:S(2)}, u32[]{:S(2)}) collective-permute-start(f32[32,128]{1,0:T(8,128)S(1)} %fusion), channel_id=1, source_target_pairs={{0,1},{1,2},{2,3},{3,4},{4,5},{5,6},{6,7},{7,8},{8,9},{9,10},{10,1... | collective-permute-start | bytes 49160
  828.6 42.7 %collective-permute-start.40 = (f32[32,128]{1,0:T(8,128)S(1)}, f32[32,128]{1,0:T(8,128)S(1)}, u32[]{:S(2)}, u32[]{:S(2)}) collective-permute-start(f32[32,128]{1,0:T(8,128)S(1)} %fusion), channel_id=1, source_target_pairs={{0,37},{1,38},{2,39},{3,40},{4,41},{5,42},{6,43},{7,44},{8,45},{9,... | collective-permute-start | bytes 49160
  838.1 37.2 %collective-permute-start.41 = (f32[32,128]{1,0:T(8,128)S(1)}, f32[32,128]{1,0:T(8,128)S(1)}, u32[]{:S(2)}, u32[]{:S(2)}) collective-permute-start(f32[32,128]{1,0:T(8,128)S(1)} %fusion), channel_id=1, source_target_pairs={{0,38},{1,39},{2,40},{3,41},{4,42},{5,43},{6,44},{7,45},{8,46},{9,... | collective-permute-start | bytes 49160
  844.1 45.7 %collective-permute-start.42 = (f32[32,128]{1,0:T(8,128)S(1)}, f32[32,128]{1,0:T(8,128)S(1)}, u32[]{:S(2)}, u32[]{:S(2)}) collective-permute-start(f32[32,128]{1,0:T(8,128)S(1)} %fusion), channel_id=1, source_target_pairs={{0,39},{1,40},{2,41},{3,42},{4,43},{5,44},{6,45},{7,46},{8,47},{9,... | collective-permute-start | bytes 49160
  849.0 53.9 %collective-permute-start.5 = (f32[32,128]{1,0:T(8,128)S(1)}, f32[32,128]{1,0:T(8,128)S(1)}, u32[]{:S(2)}, u32[]{:S(2)}) collective-permute-start(f32[32,128]{1,0:T(8,128)S(1)} %fusion), channel_id=1, source_target_pairs={{0,2},{1,3},{2,4},{3,5},{4,6},{5,7},{6,8},{7,9},{8,10},{9,11},{10,... | collective-permute-start | bytes 49160
  857.6 58.5 %collective-permute-start.6 = (f32[32,128]{1,0:T(8,128)S(1)}, f32[32,128]{1,0:T(8,128)}, u32[]{:S(2)}, u32[]{:S(2)}) collective-permute-start(f32[32,128]{1,0:T(8,128)S(1)} %fusion), channel_id=1, source_target_pairs={{0,3},{1,4},{2,5},{3,6},{4,7},{5,8},{6,9},{7,10},{8,11},{9,12},{10... | collective-permute-start | bytes 49160
  871.9 109.7 %collective-permute-start.2 = (bf16[3,256,384]{2,1,0:T(8,128)(2,1)}, bf16[3,256,384]{2,1,0:T(8,128)(2,1)}, u32[]{:S(2)}, u32[]{:S(2)}) collective-permute-start(bf16[3,256,384]{2,1,0:T(8,128)(2,1)} %bitcast.9), channel_id=1, source_target_pairs={{2,0},{3,1},{4,2},{5,3},{6,4},{7,5},{8,6},{9,7},{10,8},{11,9},{12,... | collective-permute-start | bytes 1769480 | tf_op jit(solution)/shard_map/ppermute | solution.py:14
  875.4 48.4 %collective-permute-start.7 = (f32[32,128]{1,0:T(8,128)S(1)}, f32[32,128]{1,0:T(8,128)}, u32[]{:S(2)}, u32[]{:S(2)}) collective-permute-start(f32[32,128]{1,0:T(8,128)S(1)} %fusion), channel_id=1, source_target_pairs={{0,4},{1,5},{2,6},{3,7},{4,8},{5,9},{6,10},{7,11},{8,12},{9,13},{1... | collective-permute-start | bytes 49160
  889.7 34.0 %collective-permute-start.8 = (f32[32,128]{1,0:T(8,128)S(1)}, f32[32,128]{1,0:T(8,128)}, u32[]{:S(2)}, u32[]{:S(2)}) collective-permute-start(f32[32,128]{1,0:T(8,128)S(1)} %fusion), channel_id=1, source_target_pairs={{0,5},{1,6},{2,7},{3,8},{4,9},{5,10},{6,11},{7,12},{8,13},{9,14},{... | collective-permute-start | bytes 49160
  902.9 20.9 %collective-permute-start.9 = (f32[32,128]{1,0:T(8,128)S(1)}, f32[32,128]{1,0:T(8,128)}, u32[]{:S(2)}, u32[]{:S(2)}) collective-permute-start(f32[32,128]{1,0:T(8,128)S(1)} %fusion), channel_id=1, source_target_pairs={{0,6},{1,7},{2,8},{3,9},{4,10},{5,11},{6,12},{7,13},{8,14},{9,15},... | collective-permute-start | bytes 49160
  916.1 67.6 %collective-permute-start.3 = (bf16[3,256,384]{2,1,0:T(8,128)(2,1)}, bf16[3,256,384]{2,1,0:T(8,128)(2,1)S(1)}, u32[]{:S(2)}, u32[]{:S(2)}) collective-permute-start(bf16[3,256,384]{2,1,0:T(8,128)(2,1)} %bitcast.9), channel_id=1, source_target_pairs={{0,2},{1,3},{2,4},{3,5},{4,6},{5,7},{6,8},{7,9},{8,10},{9,11},{10,... | collective-permute-start | bytes 1769480 | tf_op jit(solution)/shard_map/ppermute | solution.py:14
  (42 other events, 1554.1 us)
Sparse Core Ops, SparseCore 0:
  923.9 256.8 all-reduce.4
where the time goes:
time: 1200 us; the launch traced here: 1190 us
  blocking collectives  678 us (56%)
  waiting for transfers between devices  212 us (18%)
  starting transfers between devices  189 us (16%)
  local copies, waits for them, and re-layouts  67.3 us (6%)
  matrix products  20.6 us (2%)
  between operations  15.3 us (1%)
    unnamed x1, blocking collectives  678 us
    unnamed x42, waiting for transfers between devices  192 us
    unnamed x41, starting transfers between devices  178 us
    unnamed x94, local copies, waits for them, and re-layouts  60.4 us
  transfers between devices with their start and end apart: 45, of which 3 were waited for; matrix products, arithmetic and copies ran while one was open for 6% of the time, Pallas kernels for 0%

commit v1 on v0

v1 whole, which is shorter than its diff:
```python
import functools
import math

import jax
import jax.numpy as jnp
from jax import lax
from jax.experimental import pallas as pl
from jax.experimental.pallas import tpu as pltpu
from jax.sharding import PartitionSpec as P

MESH = pl.DeviceIdType.MESH
F32 = jnp.float32
BF16 = jnp.bfloat16
SLOPE = math.sqrt(2.0 / math.pi)
CUBIC = 0.044715

WIN = 3
BINS = 256
ROWS = WIN * BINS
C = 768
BN = 384
COL = 128
CHUNKS = BN // COL
PROJ = CHUNKS
ROUNDS = CHUNKS + 1
ALL = 2304
UNIT = 72
PART = 4 * UNIT
OWN = 9


def gelu_parts(v):
    sq = v * v
    t = jnp.tanh(SLOPE * v * (1.0 + CUBIC * sq))
    half = 0.5 * (1.0 + t)
    value = v * half
    slope = half + (0.5 * SLOPE) * v * (1.0 - t * t) * (1.0 + (3.0 * CUBIC) * sq)
    return value, slope


def dot(a, b, ca=1, cb=0):
    return lax.dot_general(a, b, (((ca,), (cb,)), ((), ())), preferred_element_type=F32)


def kernel(
    factor,
    x_hbm, w_hbm, p_hbm, g_hbm,
    out_hbm, dx_hbm, conv_ref, proj_ref,
    x_v, w_v, p_v, g_v, act, act_t, slope_x, cpre, dmid, mid, dact, out_v, dx_v,
    u_send, v_send, u_recv, v_recv, d_send, dup_recv, dlo_recv,
    total, pair_send, pair_recv, x_send, x_recv, acc, yz_send, yz_recv,
    in_sem, out_sem, ph_send_sem, u_sem, v_sem, dup_sem, dlo_sem,
    pair_ssem, pair_rsem, x_ssem, x_rsem, yz_ssem, yz_rsem,
):
    zh = lax.axis_index("dp")
    s = lax.axis_index("seq")
    x = s // 16
    zl = lax.rem(s // 8, 2)
    y = lax.rem(s // 2, 4)
    c = lax.rem(s, 2)
    off = lax.rem(zl + c, 2)

    def device(zh_, x_, zl_, y_, c_):
        return (zh_, ((x_ * 2 + zl_) * 4 + y_) * 2 + c_)

    upper = (zh, lax.rem(s + 2, 64))
    lower = (zh, lax.rem(s + 62, 64))
    sibling = device(zh, x, zl, y, 1 - c)

    loads = {}
    def load(name, src, dst, i):
        loads[name] = pltpu.make_async_copy(src, dst, in_sem.at[i])
        loads[name].start()
    load("x0", x_hbm.at[0], x_v.at[0], 0)
    load("w0", w_hbm.at[0], w_v.at[0], 3)
    load("w2", w_hbm.at[2], w_v.at[2], 5)
    load("x1", x_hbm.at[1], x_v.at[1], 1)
    load("x2", x_hbm.at[2], x_v.at[2], 2)
    load("w1", w_hbm.at[1], w_v.at[1], 4)
    load("p", p_hbm, p_v, 6)
    load("g", g_hbm, g_v, 7)

    barrier = pltpu.get_barrier_semaphore()
    def greet(peer):
        pl.semaphore_signal(barrier, inc=1, device_id=peer, device_id_type=MESH)
    greet(upper)
    greet(lower)
    greet(sibling)
    for k in (1, 2, 3):
        greet(device(zh, lax.rem(x + k, 4), zl, y, c))
    for kz in range(4):
        for ky in range(4):
            for kl in range(2):
                peer = device(lax.rem(zh + kz, 4), x, lax.rem(zl + c + kl, 2), lax.rem(y + ky, 4), zl)
                if kz == 0 and ky == 0 and kl == 0:
                    pass
                me_too = (kz == 0 and ky == 0)
                if me_too:
                    is_self = jnp.logical_and(lax.rem(zl + c + kl, 2) == zl, c == zl)
                    @pl.when(jnp.logical_not(is_self))
                    def _(peer=peer):
                        greet(peer)
                else:
                    greet(peer)

    n_far = jnp.where(off == 0, 31, 32)

    def send_halo(src, dst, sem, ssem, ch, w, to):
        pltpu.make_async_remote_copy(
            src_ref=src.at[ch, pl.ds(w * BINS, BINS)],
            dst_ref=dst.at[ch, pl.ds(w * BINS, BINS)],
            send_sem=ph_send_sem.at[ssem],
            recv_sem=sem.at[ch, w],
            device_id=to,
            device_id_type=MESH,
        ).start()

    def wait_halo(dst, sem, ch, w):
        ref = dst.at[ch, pl.ds(w * BINS, BINS)]
        pltpu.make_async_remote_copy(
            src_ref=ref, dst_ref=ref, send_sem=ph_send_sem.at[0], recv_sem=sem.at[ch, w],
            device_id=upper, device_id_type=MESH,
        ).wait_recv()

    SLAB = 16
    for w in range(WIN):
        loads["x%d" % w].wait()
        def activate(i, carry, w=w):
            r = pl.multiple_of(i * SLAB, SLAB)
            v = x_v[w, pl.ds(r, SLAB), :].astype(F32)
            value, slope = gelu_parts(v)
            act[pl.ds(w * BINS + r, SLAB), :] = value.astype(BF16)
            slope_x[pl.ds(w * BINS + r, SLAB), :] = slope
            return carry
        lax.fori_loop(0, BINS // SLAB, activate, 0)
        a_w = act[pl.ds(w * BINS, BINS), :]
        if w == 0:
            loads["w0"].wait()
        u = dot(a_w, w_v[0]).astype(BF16)
        for ch in range(CHUNKS):
            u_send[ch, pl.ds(w * BINS, BINS), :] = u[:, ch * COL:(ch + 1) * COL]
        if w == 0:
            pl.semaphore_wait(barrier, 2 + 1 + 3 + n_far)
        send_halo(u_send, u_recv, u_sem, 0, 0, w, upper)
        if w == 0:
            loads["w2"].wait()
        v = dot(a_w, w_v[2]).astype(BF16)
        for ch in range(CHUNKS):
            v_send[ch, pl.ds(w * BINS, BINS), :] = v[:, ch * COL:(ch + 1) * COL]
        send_halo(v_send, v_recv, v_sem, 1, 0, w, lower)
    for ch in range(1, CHUNKS):
        for w in range(WIN):
            send_halo(u_send, u_recv, u_sem, 0, ch, w, upper)
            send_halo(v_send, v_recv, v_sem, 1, ch, w, lower)

    loads["w1"].wait()
    loads["p"].wait()
    loads["g"].wait()
    for w in range(WIN):
        rows = pl.ds(w * BINS, BINS)
        cpre[rows, :] = dot(act[rows, :], w_v[1])
        dmid[rows, :] = dot(g_v[w], p_v[...], 1, 1)
        act_t[:, rows] = act[rows, :].T

    def clear_if(cond, ref, ch, w):
        @pl.when(cond)
        def _():
            ref[ch, pl.ds(w * BINS, BINS), :] = jnp.zeros((BINS, COL), BF16)

    MIDSLAB = 64
    for ch in range(CHUNKS):
        for w in range(WIN):
            wait_halo(u_recv, u_sem, ch, w)
            wait_halo(v_recv, v_sem, ch, w)
            clear_if(s < 2, u_recv, ch, w)
            clear_if(s >= 62, v_recv, ch, w)
            def bottleneck(i, carry, ch=ch, w=w):
                r = pl.multiple_of(w * BINS + i * MIDSLAB, MIDSLAB)
                rows = pl.ds(r, MIDSLAB)
                cols = pl.ds(ch * COL, COL)
                pre = cpre[rows, cols] + u_recv[ch, rows, :].astype(F32) + v_recv[ch, rows, :].astype(F32)
                value, slope = gelu_parts(pre)
                mid[rows, cols] = value.astype(BF16)
                d_send[ch, rows, :] = (dmid[rows, cols] * slope).astype(BF16)
                return carry
            lax.fori_loop(0, BINS // MIDSLAB, bottleneck, 0)
            send_halo(d_send, dlo_recv, dlo_sem, 2, ch, w, upper)
            send_halo(d_send, dup_recv, dup_sem, 3, ch, w, lower)
        total[ch, pl.ds(C, C), :] = dot(act_t[...], d_send[ch])

    def unit(rnd, zh_, x_, zl_):
        start = pl.multiple_of((zh_ * 8 + x_ * 2 + zl_) * UNIT, 8)
        return total[rnd, pl.ds(start, UNIT), :]

    def part(rnd, x_, zl_):
        return jnp.concatenate([unit(rnd, k, x_, zl_) for k in range(4)], axis=0)

    def pair_copy(rnd):
        return pltpu.make_async_remote_copy(
            src_ref=pair_send.at[rnd], dst_ref=pair_recv.at[rnd],
            send_sem=pair_ssem.at[rnd], recv_sem=pair_rsem.at[rnd],
            device_id=sibling, device_id_type=MESH,
        )

    def stage_a(rnd):
        for xa in range(4):
            pair_send[rnd, pl.ds(xa * PART, PART), :] = part(rnd, xa, 1 - c).astype(BF16)
        pair_copy(rnd).start()

    def x_copy(rnd, k):
        return pltpu.make_async_remote_copy(
            src_ref=x_send.at[rnd, k - 1], dst_ref=x_recv.at[rnd, k - 1],
            send_sem=x_ssem.at[rnd, k - 1], recv_sem=x_rsem.at[rnd, k - 1],
            device_id=device(zh, lax.rem(x + k, 4), zl, y, c), device_id_type=MESH,
        )

    def stage_b(rnd):
        pair_copy(rnd).wait_recv()
        for k in (2, 1, 3, 0):
            xa = lax.rem(x + k, 4)
            other = pair_recv[rnd, pl.ds(pl.multiple_of(xa * PART, 16), PART), :]
            both = part(rnd, xa, c) + other.astype(F32)
            if k:
                x_send[rnd, k - 1] = both.astype(BF16)
                x_copy(rnd, k).start()
            else:
                acc[rnd, pl.ds(0, PART), :] = both
                acc[rnd, pl.ds(PART, 16), :] = jnp.zeros((16, COL), F32)

    def far_copy(rnd, kz, ky, kc):
        za = lax.rem(zh + kz, 4)
        ya = lax.rem(y + ky, 4)
        ca = lax.rem(c + kc, 2)
        return pltpu.make_async_remote_copy(
            src_ref=yz_send.at[rnd, (za * 4 + ya) * 2 + ca],
            dst_ref=yz_recv.at[rnd, (kz * 4 + ky) * 2 + off],
            send_sem=yz_ssem.at[rnd], recv_sem=yz_rsem.at[rnd],
            device_id=device(za, x, c, ya, ca), device_id_type=MESH,
        )

    def stage_c(rnd):
        for k in (1, 3, 2):
            x_copy(rnd, k).wait_recv()
        acc[rnd, pl.ds(0, PART), :] = (
            acc[rnd, pl.ds(0, PART), :] + x_recv[rnd, 0].astype(F32)
            + x_recv[rnd, 1].astype(F32) + x_recv[rnd, 2].astype(F32)
        )
        for b in range(32):
            yz_send[rnd, b] = acc[rnd, pl.ds(OWN * b, 16), :].astype(BF16)
        for kz in (2, 1, 3, 0):
            for ky in (2, 1, 3, 0):
                for kc in (1, 0):
                    if kz == 0 and ky == 0 and kc == 0:
                        @pl.when(off == 0)
                        def _():
                            yz_recv[rnd, 0] = yz_send[rnd, (zh * 4 + y) * 2 + c]
                        @pl.when(off == 1)
                        def _():
                            far_copy(rnd, 0, 0, 0).start()
                    else:
                        far_copy(rnd, kz, ky, kc).start()

    def far_wait(rnd, first, recv):
        ref = yz_recv.at[rnd, pl.ds(first, 32 - first)]
        copy = pltpu.make_async_remote_copy(
            src_ref=yz_send.at[rnd, pl.ds(first, 32 - first)], dst_ref=ref,
            send_sem=yz_ssem.at[rnd], recv_sem=yz_rsem.at[rnd],
            device_id=sibling, device_id_type=MESH,
        )
        if recv:
            copy.wait_recv()
        else:
            copy.wait_send()

    def far_wait_all(rnd, recv):
        @pl.when(off == 0)
        def _():
            far_wait(rnd, 1, recv)
        @pl.when(off == 1)
        def _():
            far_wait(rnd, 0, recv)

    def stage_d(rnd):
        far_wait_all(rnd, True)
        result = jnp.sum(yz_recv[rnd].astype(F32), axis=0)[:OWN] * factor
        if rnd == PROJ:
            proj_ref[...] = result
        else:
            conv_ref[pl.ds(rnd, OWN, stride=CHUNKS), :] = result

    grad = dot(mid[pl.ds(0, BINS), :], g_v[0], 0, 0)
    for w in range(1, WIN):
        grad = grad + dot(mid[pl.ds(w * BINS, BINS), :], g_v[w], 0, 0)
    for j in range(C // COL):
        total[PROJ, pl.ds(j, BN, stride=C // COL), :] = grad[:, j * COL:(j + 1) * COL]
    stage_a(PROJ)
    stores = []
    for w in range(WIN):
        rows = pl.ds(w * BINS, BINS)
        out_v[w] = (x_v[w].astype(F32) + dot(mid[rows, :], p_v[...])).astype(BF16)
    stores.append(pltpu.make_async_copy(out_v, out_hbm, out_sem.at[0]))
    stores[0].start()
    stage_b(PROJ)

    def outer_taps(ch):
        for w in range(WIN):
            wait_halo(dup_recv, dup_sem, ch, w)
            wait_halo(dlo_recv, dlo_sem, ch, w)
            clear_if(s < 2, dlo_recv, ch, w)
            clear_if(s >= 62, dup_recv, ch, w)
        total[ch, pl.ds(0, C), :] = dot(act_t[...], dup_recv[ch])
        total[ch, pl.ds(2 * C, C), :] = dot(act_t[...], dlo_recv[ch])

    def input_side(ch):
        cols = pl.ds(ch * COL, COL)
        for w in range(WIN):
            rows = pl.ds(w * BINS, BINS)
            term = (
                dot(dup_recv[ch, rows, :], w_v[0, :, cols], 1, 1)
                + dot(d_send[ch, rows, :], w_v[1, :, cols], 1, 1)
                + dot(dlo_recv[ch, rows, :], w_v[2, :, cols], 1, 1)
            )
            if ch:
                term = term + dact[rows, :]
            if ch < CHUNKS - 1:
                dact[rows, :] = term
            else:
                dx_v[w] = (g_v[w].astype(F32) + term * slope_x[rows, :]).astype(BF16)

    outer_taps(0)
    stage_a(0)
    stage_c(PROJ)
    input_side(0)
    stage_b(0)
    outer_taps(1)
    stage_a(1)
    stage_c(0)
    stage_d(PROJ)
    input_side(1)
    stage_b(1)
    outer_taps(2)
    stage_a(2)
    stage_c(1)
    stage_b(2)
    input_side(2)
    stores.append(pltpu.make_async_copy(dx_v, dx_hbm, out_sem.at[1]))
    stores[1].start()
    stage_d(0)
    stage_c(2)
    stage_d(1)

    for i, (ref, to) in enumerate(((u_send, upper), (v_send, lower), (d_send, upper), (d_send, lower))):
        pltpu.make_async_remote_copy(
            src_ref=ref, dst_ref=ref, send_sem=ph_send_sem.at[i], recv_sem=u_sem.at[0, 0],
            device_id=to, device_id_type=MESH,
        ).wait_send()
    for rnd in range(ROUNDS):
        pair_copy(rnd).wait_send()
        for k in (1, 2, 3):
            x_copy(rnd, k).wait_send()
        far_wait_all(rnd, False)
    stage_d(2)
    for copy in stores:
        copy.wait()


def local(inputs, dilated_tap_weight, proj_weight, cotangent):
    total_rows = inputs.shape[0] * lax.axis_size("dp") * inputs.shape[1] * lax.axis_size("seq")
    factor = 1.0 / math.sqrt(total_rows)
    vm = pltpu.VMEM
    dma = pltpu.SemaphoreType.DMA
    halo = (CHUNKS, ROWS, COL)
    hbm = pl.BlockSpec(memory_space=pl.ANY)
    vmem = pl.BlockSpec(memory_space=pltpu.VMEM)
    return pl.pallas_call(
        functools.partial(kernel, factor),
        out_shape=(
            jax.ShapeDtypeStruct(inputs.shape, BF16),
            jax.ShapeDtypeStruct(inputs.shape, BF16),
            jax.ShapeDtypeStruct((CHUNKS * OWN, COL), F32),
            jax.ShapeDtypeStruct((OWN, COL), F32),
        ),
        in_specs=[hbm] * 4,
        out_specs=(hbm, hbm, vmem, vmem),
        scratch_shapes=[
            vm((WIN, BINS, C), BF16), vm((3, C, BN), BF16), vm((BN, C), BF16), vm((WIN, BINS, C), BF16),
            vm((ROWS, C), BF16), vm((C, ROWS), BF16), vm((ROWS, C), F32),
            vm((ROWS, BN), F32), vm((ROWS, BN), F32), vm((ROWS, BN), BF16), vm((ROWS, C), F32),
            vm((WIN, BINS, C), BF16), vm((WIN, BINS, C), BF16),
            vm(halo, BF16), vm(halo, BF16), vm(halo, BF16), vm(halo, BF16),
            vm(halo, BF16), vm(halo, BF16), vm(halo, BF16),
            vm((ROUNDS, ALL, COL), F32),
            vm((ROUNDS, 4 * PART, COL), BF16), vm((ROUNDS, 4 * PART, COL), BF16),
            vm((ROUNDS, 3, PART, COL), BF16), vm((ROUNDS, 3, PART, COL), BF16),
            vm((ROUNDS, PART + 16, COL), F32),
            vm((ROUNDS, 32, 16, COL), BF16), vm((ROUNDS, 32, 16, COL), BF16),
            dma((8,)), dma((2,)), dma((4,)),
            dma((CHUNKS, WIN)), dma((CHUNKS, WIN)), dma((CHUNKS, WIN)), dma((CHUNKS, WIN)),
            dma((ROUNDS,)), dma((ROUNDS,)), dma((ROUNDS, 3)), dma((ROUNDS, 3)),
            dma((ROUNDS,)), dma((ROUNDS,)),
        ],
        compiler_params=pltpu.CompilerParams(
            collective_id=0, has_side_effects=True, vmem_limit_bytes=56 * 1024 * 1024
        ),
        name="block",
    )(inputs, dilated_tap_weight, proj_weight, cotangent)


def solution(mesh):
    return jax.shard_map(
        local,
        mesh=mesh,
        in_specs=(P("dp", "seq", None), P(), P(), P("dp", "seq", None)),
        out_specs=(
            P("dp", "seq", None),
            P("dp", "seq", None),
            P(("dp", "seq"), None),
            P(("dp", "seq"), None),
        ),
        check_vma=False,
    )
```

time: 1200 us -> 74.3 us (0.06)
  blocking collectives: 678 us -> 0 us
  waiting for transfers between devices: 212 us -> 0 us
  starting transfers between devices: 189 us -> 0 us
  Pallas kernels: 0 us -> 68.9 us
  local copies, waits for them, and re-layouts: 67.3 us -> 4.68 us
  matrix products: 20.6 us -> 0 us
  between operations: 15.3 us -> 0.65 us
    unnamed x1 -> x0, blocking collectives: 678 us -> none
    unnamed x42 -> x0, waiting for transfers between devices: 192 us -> none
    unnamed x41 -> x0, starting transfers between devices: 178 us -> none
    pallas_call x0 -> x1, Pallas kernels: none -> 68.9 us  [local(): pl.pallas_call(functools.partial(kernel, factor), out_shape=(jax.ShapeDty...]
    unnamed x94 -> x10, local copies, waits for them, and re-layouts: 60.4 us -> 4.68 us
    dot_general x12 -> x0, matrix products: 20.6 us -> none  [the longest x3 6 us: block_pass(): jnp.dot(tap.T, preactivation_gradient, preferred_element_type=jnp.float32)]
    ppermute x4 -> x0, waiting for transfers between devices: 19.5 us -> none  [from_behind(): return lax.ppermute(block, axis, route)]
  transfers between devices with their start and end apart: 45 -> 0, of which waited for: 3 -> 0; matrix products, arithmetic and copies ran while one was open for 6% -> 0% of each run, Pallas kernels for 0% -> 0%
where the time goes in v1:
time: 74.3 us; the launch traced here: 74.2 us
  Pallas kernels  68.9 us (93%)
  local copies, waits for them, and re-layouts  4.68 us (6%)
    pallas_call x1, Pallas kernels, local(): pl.pallas_call(functools.partial(kernel, factor), out_shape=(jax.ShapeDty...  68.9 us
    unnamed x10, local copies, waits for them, and re-layouts  4.68 us

profile of v1, /device:TPU:1, one launch (start us, length us, event | category | flops | bytes accessed | tf_op | source)
XLA Modules:
  0.0 74.2 jit_solution(15092927027614585193)
XLA Ops:
  0.6 68.9 %block.1 = (bf16[3,256,768]{2,1,0:T(8,128)(2,1)}, bf16[3,256,768]{2,1,0:T(8,128)(2,1)}, f32[27,128]{1,0:T(8,128)}, f32[9,128]{1,0:T(8,128)}) custom-call(bf16[3,256,768]{2,1,0:T(8,128)(2,1)} %x_hbm.1, bf16[3,768,384]{2,1,0:T(8,128)(2,1)} %w_hbm.1, bf16[384,768]{1,0:T(8,128)(2,1)} %p_hbm.1, bf16[3,256,768]{2,1,0:T(8,128)(2,1)} %g_hbm.1), custom_call_target="tpu_custom_call" | custom-call | tf_op jit(solution)/shard_map/block/pallas_call | solution.py:375
  69.5 0.0 copy-start
  69.5 2.5 %copy.12 = bf16[3,256,768]{2,1,0:T(8,128)(2,1)} copy(bf16[3,256,768]{2,1,0:T(8,128)(2,1)} %get-tuple-element.8) | data formatting | bytes 2359296
  72.0 0.0 copy-done
  72.0 0.0 copy-start.1
  72.0 0.0 copy-start.2
  72.0 1.0 %copy.13 = bf16[3,256,768]{2,1,0:T(8,128)(2,1)} copy(bf16[3,256,768]{2,1,0:T(8,128)(2,1)S(1)} %copy-done) | data formatting | bytes 2359296
  73.0 0.0 copy-done.1
  73.0 0.6 copy.14
  73.6 0.0 copy-done.2
  73.6 0.6 copy.15
Async XLA Ops:
  69.5 2.5 %copy-start = (bf16[3,256,768]{2,1,0:T(8,128)(2,1)S(1)}, bf16[3,256,768]{2,1,0:T(8,128)(2,1)}, u32[]{:S(2)}) copy-start(bf16[3,256,768]{2,1,0:T(8,128)(2,1)} %get-tuple-element.9) | copy-start | bytes 3538948
  72.0 1.0 %copy-start.1 = (f32[27,128]{1,0:T(8,128)S(1)}, f32[27,128]{1,0:T(8,128)}, u32[]{:S(2)}) copy-start(f32[27,128]{1,0:T(8,128)} %get-tuple-element.10) | copy-start | bytes 41476
  72.0 1.6 %copy-start.2 = (f32[9,128]{1,0:T(8,128)S(1)}, f32[9,128]{1,0:T(8,128)}, u32[]{:S(2)}) copy-start(f32[9,128]{1,0:T(8,128)} %get-tuple-element.11) | copy-start | bytes 13828

commit v2 on v1

--- a/solution.py
+++ b/solution.py
@@ -23,9 +23,11 @@
 CHUNKS = BN // COL
 PROJ = CHUNKS
 ROUNDS = CHUNKS + 1
+LAST = CHUNKS - 1
 ALL = 2304
 UNIT = 72
 PART = 4 * UNIT
+LINE = 18
 OWN = 9
 
 
@@ -48,9 +50,10 @@
     out_hbm, dx_hbm, conv_ref, proj_ref,
     x_v, w_v, p_v, g_v, act, act_t, slope_x, cpre, dmid, mid, dact, out_v, dx_v,
     u_send, v_send, u_recv, v_recv, d_send, dup_recv, dlo_recv,
-    total, pair_send, pair_recv, x_send, x_recv, acc, yz_send, yz_recv,
+    total, pair_send, pair_recv, x_send, x_recv, acc,
+    y_sum, y_send, y_recv, z_sum, z_send, z_recv,
     in_sem, out_sem, ph_send_sem, u_sem, v_sem, dup_sem, dlo_sem,
-    pair_ssem, pair_rsem, x_ssem, x_rsem, yz_ssem, yz_rsem,
+    pair_ssem, pair_rsem, x_ssem, x_rsem, y_ssem, y_rsem, z_ssem, z_rsem,
 ):
     zh = lax.axis_index("dp")
     s = lax.axis_index("seq")
@@ -88,22 +91,17 @@
     greet(sibling)
     for k in (1, 2, 3):
         greet(device(zh, lax.rem(x + k, 4), zl, y, c))
+        greet(device(zh, x, zl, lax.rem(y + k, 4), c))
     for kz in range(4):
-        for ky in range(4):
-            for kl in range(2):
-                peer = device(lax.rem(zh + kz, 4), x, lax.rem(zl + c + kl, 2), lax.rem(y + ky, 4), zl)
-                if kz == 0 and ky == 0 and kl == 0:
-                    pass
-                me_too = (kz == 0 and ky == 0)
-                if me_too:
-                    is_self = jnp.logical_and(lax.rem(zl + c + kl, 2) == zl, c == zl)
-                    @pl.when(jnp.logical_not(is_self))
-                    def _(peer=peer):
-                        greet(peer)
-                else:
+        for kl in range(2):
+            peer = device(lax.rem(zh + kz, 4), x, lax.rem(zl + c + kl, 2), y, zl)
+            if kz == 0:
+                is_self = jnp.logical_and(lax.rem(c + kl, 2) == 0, c == zl)
+                @pl.when(jnp.logical_not(is_self))
+                def _(peer=peer):
                     greet(peer)
-
-    n_far = jnp.where(off == 0, 31, 32)
+            else:
+                greet(peer)
 
     def send_halo(src, dst, sem, ssem, ch, w, to):
         pltpu.make_async_remote_copy(
@@ -140,7 +138,7 @@
         for ch in range(CHUNKS):
             u_send[ch, pl.ds(w * BINS, BINS), :] = u[:, ch * COL:(ch + 1) * COL]
         if w == 0:
-            pl.semaphore_wait(barrier, 2 + 1 + 3 + n_far)
+            pl.semaphore_wait(barrier, 2 + 1 + 3 + 3 + 7 + off)
         send_halo(u_send, u_recv, u_sem, 0, 0, w, upper)
         if w == 0:
             loads["w2"].wait()
@@ -148,10 +146,13 @@
         for ch in range(CHUNKS):
             v_send[ch, pl.ds(w * BINS, BINS), :] = v[:, ch * COL:(ch + 1) * COL]
         send_halo(v_send, v_recv, v_sem, 1, 0, w, lower)
-    for ch in range(1, CHUNKS):
+
+    def send_products(ch):
         for w in range(WIN):
             send_halo(u_send, u_recv, u_sem, 0, ch, w, upper)
             send_halo(v_send, v_recv, v_sem, 1, ch, w, lower)
+
+    send_products(1)
 
     loads["w1"].wait()
     loads["p"].wait()
@@ -168,13 +169,13 @@
             ref[ch, pl.ds(w * BINS, BINS), :] = jnp.zeros((BINS, COL), BF16)
 
     MIDSLAB = 64
-    for ch in range(CHUNKS):
+    def middle(ch):
         for w in range(WIN):
             wait_halo(u_recv, u_sem, ch, w)
             wait_halo(v_recv, v_sem, ch, w)
             clear_if(s < 2, u_recv, ch, w)
             clear_if(s >= 62, v_recv, ch, w)
-            def bottleneck(i, carry, ch=ch, w=w):
+            def bottleneck(i, carry, w=w):
                 r = pl.multiple_of(w * BINS + i * MIDSLAB, MIDSLAB)
                 rows = pl.ds(r, MIDSLAB)
                 cols = pl.ds(ch * COL, COL)
@@ -186,6 +187,8 @@
             lax.fori_loop(0, BINS // MIDSLAB, bottleneck, 0)
             send_halo(d_send, dlo_recv, dlo_sem, 2, ch, w, upper)
             send_halo(d_send, dup_recv, dup_sem, 3, ch, w, lower)
+
+    def centre_tap(ch):
         total[ch, pl.ds(C, C), :] = dot(act_t[...], d_send[ch])
 
     def unit(rnd, zh_, x_, zl_):
@@ -214,93 +217,135 @@
             device_id=device(zh, lax.rem(x + k, 4), zl, y, c), device_id_type=MESH,
         )
 
-    def stage_b(rnd):
+    def both_cores(rnd, xa):
+        other = pair_recv[rnd, pl.ds(pl.multiple_of(xa * PART, 16), PART), :]
+        return part(rnd, xa, c) + other.astype(F32)
+
+    step = jnp.where(zl == 1, 1, 3)
+
+    def ring_copy(rnd, t):
+        return pltpu.make_async_remote_copy(
+            src_ref=x_send.at[rnd, t], dst_ref=x_recv.at[rnd, t],
+            send_sem=x_ssem.at[rnd, t], recv_sem=x_rsem.at[rnd, t],
+            device_id=device(zh, lax.rem(x + step, 4), zl, y, c), device_id_type=MESH,
+        )
+
+    def ring(rnd, t):
+        if t == 0:
+            pair_copy(rnd).wait_recv()
+            part_sum = both_cores(rnd, lax.rem(x + 4 - step, 4))
+        else:
+            ring_copy(rnd, t - 1).wait_recv()
+            xa = lax.rem(x + 2, 4) if t == 1 else lax.rem(x + step, 4)
+            part_sum = both_cores(rnd, xa) + x_recv[rnd, t - 1].astype(F32)
+        x_send[rnd, t] = part_sum.astype(BF16)
+        ring_copy(rnd, t).start()
+
+    def straight(rnd):
         pair_copy(rnd).wait_recv()
-        for k in (2, 1, 3, 0):
-            xa = lax.rem(x + k, 4)
-            other = pair_recv[rnd, pl.ds(pl.multiple_of(xa * PART, 16), PART), :]
-            both = part(rnd, xa, c) + other.astype(F32)
-            if k:
-                x_send[rnd, k - 1] = both.astype(BF16)
-                x_copy(rnd, k).start()
-            else:
-                acc[rnd, pl.ds(0, PART), :] = both
-                acc[rnd, pl.ds(PART, 16), :] = jnp.zeros((16, COL), F32)
-
-    def far_copy(rnd, kz, ky, kc):
+        for k in (2, 1, 3):
+            x_send[rnd, k - 1] = both_cores(rnd, lax.rem(x + k, 4)).astype(BF16)
+            x_copy(rnd, k).start()
+
+    def y_copy(rnd, k):
+        return pltpu.make_async_remote_copy(
+            src_ref=y_send.at[rnd, k - 1], dst_ref=y_recv.at[rnd, k - 1],
+            send_sem=y_ssem.at[rnd, k - 1], recv_sem=y_rsem.at[rnd, k - 1],
+            device_id=device(zh, x, zl, lax.rem(y + k, 4), c), device_id_type=MESH,
+        )
+
+    def along_y(rnd):
+        mine = both_cores(rnd, x)
+        if rnd == LAST:
+            for k in (1, 3, 2):
+                x_copy(rnd, k).wait_recv()
+            mine = mine + x_recv[rnd, 0].astype(F32) + x_recv[rnd, 1].astype(F32)
+        else:
+            ring_copy(rnd, 2).wait_recv()
+        acc[rnd] = mine + x_recv[rnd, 2].astype(F32)
+        for ya in range(4):
+            for za in range(4):
+                y_sum[rnd, ya, pl.ds(za * LINE, LINE), :] = acc[rnd, pl.ds(za * UNIT + ya * LINE, LINE), :]
+            y_sum[rnd, ya, pl.ds(UNIT, 8), :] = jnp.zeros((8, COL), F32)
+        for k in (2, 1, 3):
+            y_send[rnd, k - 1] = y_sum[rnd, lax.rem(y + k, 4)].astype(BF16)
+            y_copy(rnd, k).start()
+
+    def z_copy(rnd, kz, kc):
         za = lax.rem(zh + kz, 4)
-        ya = lax.rem(y + ky, 4)
         ca = lax.rem(c + kc, 2)
         return pltpu.make_async_remote_copy(
-            src_ref=yz_send.at[rnd, (za * 4 + ya) * 2 + ca],
-            dst_ref=yz_recv.at[rnd, (kz * 4 + ky) * 2 + off],
-            send_sem=yz_ssem.at[rnd], recv_sem=yz_rsem.at[rnd],
-            device_id=device(za, x, c, ya, ca), device_id_type=MESH,
-        )
-
-    def stage_c(rnd):
+            src_ref=z_send.at[rnd, za * 2 + ca], dst_ref=z_recv.at[rnd, kz * 2 + off],
+            send_sem=z_ssem.at[rnd], recv_sem=z_rsem.at[rnd],
+            device_id=device(za, x, c, y, ca), device_id_type=MESH,
+        )
+
+    def along_z(rnd):
         for k in (1, 3, 2):
-            x_copy(rnd, k).wait_recv()
-        acc[rnd, pl.ds(0, PART), :] = (
-            acc[rnd, pl.ds(0, PART), :] + x_recv[rnd, 0].astype(F32)
-            + x_recv[rnd, 1].astype(F32) + x_recv[rnd, 2].astype(F32)
-        )
-        for b in range(32):
-            yz_send[rnd, b] = acc[rnd, pl.ds(OWN * b, 16), :].astype(BF16)
+            y_copy(rnd, k).wait_recv()
+        z_sum[rnd] = (
+            y_sum[rnd, y] + y_recv[rnd, 0].astype(F32)
+            + y_recv[rnd, 1].astype(F32) + y_recv[rnd, 2].astype(F32)
+        )
+        for b in range(8):
+            z_send[rnd, b] = z_sum[rnd, pl.ds(OWN * b, 16), :].astype(BF16)
         for kz in (2, 1, 3, 0):
-            for ky in (2, 1, 3, 0):
-                for kc in (1, 0):
-                    if kz == 0 and ky == 0 and kc == 0:
-                        @pl.when(off == 0)
-                        def _():
-                            yz_recv[rnd, 0] = yz_send[rnd, (zh * 4 + y) * 2 + c]
-                        @pl.when(off == 1)
-                        def _():
-                            far_copy(rnd, 0, 0, 0).start()
-                    else:
-                        far_copy(rnd, kz, ky, kc).start()
-
-    def far_wait(rnd, first, recv):
-        ref = yz_recv.at[rnd, pl.ds(first, 32 - first)]
-        copy = pltpu.make_async_remote_copy(
-            src_ref=yz_send.at[rnd, pl.ds(first, 32 - first)], dst_ref=ref,
-            send_sem=yz_ssem.at[rnd], recv_sem=yz_rsem.at[rnd],
-            device_id=sibling, device_id_type=MESH,
-        )
-        if recv:
-            copy.wait_recv()
-        else:
-            copy.wait_send()
-
-    def far_wait_all(rnd, recv):
+            for kc in (1, 0):
+                if kz == 0 and kc == 0:
+                    @pl.when(off == 0)
+                    def _():
+                        z_recv[rnd, 0] = z_send[rnd, zh * 2 + c]
+                    @pl.when(off == 1)
+                    def _():
+                        z_copy(rnd, 0, 0).start()
+                else:
+                    z_copy(rnd, kz, kc).start()
+
+    def z_wait(rnd, recv):
+        def wait(first):
+            copy = pltpu.make_async_remote_copy(
+                src_ref=z_send.at[rnd, pl.ds(first, 8 - first)],
+                dst_ref=z_recv.at[rnd, pl.ds(first, 8 - first)],
+                send_sem=z_ssem.at[rnd], recv_sem=z_rsem.at[rnd],
+                device_id=sibling, device_id_type=MESH,
+            )
+            if recv:
+                copy.wait_recv()
+            else:
+                copy.wait_send()
         @pl.when(off == 0)
         def _():
-            far_wait(rnd, 1, recv)
+            wait(1)
         @pl.when(off == 1)
         def _():
-            far_wait(rnd, 0, recv)
-
-    def stage_d(rnd):
-        far_wait_all(rnd, True)
-        result = jnp.sum(yz_recv[rnd].astype(F32), axis=0)[:OWN] * factor
+            wait(0)
+
+    def finish(rnd):
+        z_wait(rnd, True)
+        result = jnp.sum(z_recv[rnd].astype(F32), axis=0)[:OWN] * factor
         if rnd == PROJ:
             proj_ref[...] = result
         else:
             conv_ref[pl.ds(rnd, OWN, stride=CHUNKS), :] = result
 
-    grad = dot(mid[pl.ds(0, BINS), :], g_v[0], 0, 0)
-    for w in range(1, WIN):
-        grad = grad + dot(mid[pl.ds(w * BINS, BINS), :], g_v[w], 0, 0)
-    for j in range(C // COL):
-        total[PROJ, pl.ds(j, BN, stride=C // COL), :] = grad[:, j * COL:(j + 1) * COL]
-    stage_a(PROJ)
+    def projection():
+        grad = dot(mid[pl.ds(0, BINS), :], g_v[0], 0, 0)
+        for w in range(1, WIN):
+            grad = grad + dot(mid[pl.ds(w * BINS, BINS), :], g_v[w], 0, 0)
+        for j in range(C // COL):
+            total[PROJ, pl.ds(j, BN, stride=C // COL), :] = grad[:, j * COL:(j + 1) * COL]
+
     stores = []
-    for w in range(WIN):
-        rows = pl.ds(w * BINS, BINS)
-        out_v[w] = (x_v[w].astype(F32) + dot(mid[rows, :], p_v[...])).astype(BF16)
-    stores.append(pltpu.make_async_copy(out_v, out_hbm, out_sem.at[0]))
-    stores[0].start()
-    stage_b(PROJ)
+    def store(src, dst):
+        copy = pltpu.make_async_copy(src, dst, out_sem.at[len(stores)])
+        copy.start()
+        stores.append(copy)
+
+    def block_output():
+        for w in range(WIN):
+            rows = pl.ds(w * BINS, BINS)
+            out_v[w] = (x_v[w].astype(F32) + dot(mid[rows, :], p_v[...])).astype(BF16)
+        store(out_v, out_hbm)
 
     def outer_taps(ch):
         for w in range(WIN):
@@ -327,27 +372,47 @@
             else:
                 dx_v[w] = (g_v[w].astype(F32) + term * slope_x[rows, :]).astype(BF16)
 
+    middle(0)
+    send_products(2)
+    centre_tap(0)
+    middle(1)
+    centre_tap(1)
     outer_taps(0)
     stage_a(0)
-    stage_c(PROJ)
     input_side(0)
-    stage_b(0)
+    ring(0, 0)
+    middle(2)
+    centre_tap(2)
+    ring(0, 1)
+    projection()
+    stage_a(PROJ)
+    block_output()
+    ring(PROJ, 0)
+    ring(0, 2)
     outer_taps(1)
     stage_a(1)
-    stage_c(0)
-    stage_d(PROJ)
+    ring(PROJ, 1)
     input_side(1)
-    stage_b(1)
+    ring(1, 0)
+    ring(PROJ, 2)
     outer_taps(2)
     stage_a(2)
-    stage_c(1)
-    stage_b(2)
+    ring(1, 1)
+    along_y(0)
+    along_y(PROJ)
+    straight(2)
+    ring(1, 2)
     input_side(2)
-    stores.append(pltpu.make_async_copy(dx_v, dx_hbm, out_sem.at[1]))
-    stores[1].start()
-    stage_d(0)
-    stage_c(2)
-    stage_d(1)
+    store(dx_v, dx_hbm)
+    along_z(0)
+    along_z(PROJ)
+    along_y(1)
+    along_y(2)
+    along_z(1)
+    finish(0)
+    finish(PROJ)
+    along_z(2)
+    finish(1)
 
     for i, (ref, to) in enumerate(((u_send, upper), (v_send, lower), (d_send, upper), (d_send, lower))):
         pltpu.make_async_remote_copy(
@@ -358,8 +423,9 @@
         pair_copy(rnd).wait_send()
         for k in (1, 2, 3):
             x_copy(rnd, k).wait_send()
-        far_wait_all(rnd, False)
-    stage_d(2)
+            y_copy(rnd, k).wait_send()
+        z_wait(rnd, False)
+    finish(LAST)
     for copy in stores:
         copy.wait()
 
@@ -392,11 +458,15 @@
             vm((ROUNDS, ALL, COL), F32),
             vm((ROUNDS, 4 * PART, COL), BF16), vm((ROUNDS, 4 * PART, COL), BF16),
             vm((ROUNDS, 3, PART, COL), BF16), vm((ROUNDS, 3, PART, COL), BF16),
-            vm((ROUNDS, PART + 16, COL), F32),
-            vm((ROUNDS, 32, 16, COL), BF16), vm((ROUNDS, 32, 16, COL), BF16),
+            vm((ROUNDS, PART, COL), F32),
+            vm((ROUNDS, 4, UNIT + 8, COL), F32),
+            vm((ROUNDS, 3, UNIT + 8, COL), BF16), vm((ROUNDS, 3, UNIT + 8, COL), BF16),
+            vm((ROUNDS, UNIT + 8, COL), F32),
+            vm((ROUNDS, 8, 16, COL), BF16), vm((ROUNDS, 8, 16, COL), BF16),
             dma((8,)), dma((2,)), dma((4,)),
             dma((CHUNKS, WIN)), dma((CHUNKS, WIN)), dma((CHUNKS, WIN)), dma((CHUNKS, WIN)),
             dma((ROUNDS,)), dma((ROUNDS,)), dma((ROUNDS, 3)), dma((ROUNDS, 3)),
+            dma((ROUNDS, 3)), dma((ROUNDS, 3)),
             dma((ROUNDS,)), dma((ROUNDS,)),
         ],
         compiler_params=pltpu.CompilerParams(

time: 74.3 us -> 70.1 us (0.943)
  Pallas kernels: 68.9 us -> 64.6 us
    pallas_call x1, Pallas kernels: 68.9 us -> 64.6 us  [local(): pl.pallas_call(functools.partial(kernel, factor), out_shape=(jax.ShapeDty...]
where the time goes in v2:
time: 70.1 us; the launch traced here: 70 us
  Pallas kernels  64.6 us (92%)
  local copies, waits for them, and re-layouts  4.68 us (7%)
    pallas_call x1, Pallas kernels, local(): pl.pallas_call(functools.partial(kernel, factor), out_shape=(jax.ShapeDty...  64.6 us
    unnamed x10, local copies, waits for them, and re-layouts  4.68 us

profile of v2, /device:TPU:1, one launch (start us, length us, event | category | flops | bytes accessed | tf_op | source)
XLA Modules:
  0.0 70.0 jit_solution(13641233599552242786)
XLA Ops:
  0.6 64.6 %block.1 = (bf16[3,256,768]{2,1,0:T(8,128)(2,1)}, bf16[3,256,768]{2,1,0:T(8,128)(2,1)}, f32[27,128]{1,0:T(8,128)}, f32[9,128]{1,0:T(8,128)}) custom-call(bf16[3,256,768]{2,1,0:T(8,128)(2,1)} %x_hbm.1, bf16[3,768,384]{2,1,0:T(8,128)(2,1)} %w_hbm.1, bf16[384,768]{1,0:T(8,128)(2,1)} %p_hbm.1, bf16[3,256,768]{2,1,0:T(8,128)(2,1)} %g_hbm.1), custom_call_target="tpu_custom_call" | custom-call | tf_op jit(solution)/shard_map/block/pallas_call | solution.py:441
  65.3 0.0 copy-start
  65.3 2.5 %copy.12 = bf16[3,256,768]{2,1,0:T(8,128)(2,1)} copy(bf16[3,256,768]{2,1,0:T(8,128)(2,1)} %get-tuple-element.8) | data formatting | bytes 2359296
  67.7 0.0 copy-done
  67.7 0.0 copy-start.1
  67.7 0.0 copy-start.2
  67.7 1.0 %copy.13 = bf16[3,256,768]{2,1,0:T(8,128)(2,1)} copy(bf16[3,256,768]{2,1,0:T(8,128)(2,1)S(1)} %copy-done) | data formatting | bytes 2359296
  68.7 0.0 copy-done.1
  68.7 0.6 copy.14
  69.3 0.0 copy-done.2
  69.4 0.6 copy.15
Async XLA Ops:
  65.3 2.5 %copy-start = (bf16[3,256,768]{2,1,0:T(8,128)(2,1)S(1)}, bf16[3,256,768]{2,1,0:T(8,128)(2,1)}, u32[]{:S(2)}) copy-start(bf16[3,256,768]{2,1,0:T(8,128)(2,1)} %get-tuple-element.9) | copy-start | bytes 3538948
  67.7 1.0 %copy-start.1 = (f32[27,128]{1,0:T(8,128)S(1)}, f32[27,128]{1,0:T(8,128)}, u32[]{:S(2)}) copy-start(f32[27,128]{1,0:T(8,128)} %get-tuple-element.10) | copy-start | bytes 41476
  67.7 1.6 %copy-start.2 = (f32[9,128]{1,0:T(8,128)S(1)}, f32[9,128]{1,0:T(8,128)}, u32[]{:S(2)}) copy-start(f32[9,128]{1,0:T(8,128)} %get-tuple-element.11) | copy-start | bytes 13828

commit v3 on v2

--- a/solution.py
+++ b/solution.py
@@ -47,12 +47,12 @@
 def kernel(
     factor,
     x_hbm, w_hbm, p_hbm, g_hbm,
-    out_hbm, dx_hbm, conv_ref, proj_ref,
-    x_v, w_v, p_v, g_v, act, act_t, slope_x, cpre, dmid, mid, dact, out_v, dx_v,
+    out_v, dx_v, conv_ref, proj_ref,
+    x_v, w_v, p_v, g_v, act, act_t, slope_x, cpre, dmid, mid, dact,
     u_send, v_send, u_recv, v_recv, d_send, dup_recv, dlo_recv,
     total, pair_send, pair_recv, x_send, x_recv, acc,
     y_sum, y_send, y_recv, z_sum, z_send, z_recv,
-    in_sem, out_sem, ph_send_sem, u_sem, v_sem, dup_sem, dlo_sem,
+    in_sem, ph_send_sem, u_sem, v_sem, dup_sem, dlo_sem,
     pair_ssem, pair_rsem, x_ssem, x_rsem, y_ssem, y_rsem, z_ssem, z_rsem,
 ):
     zh = lax.axis_index("dp")
@@ -335,17 +335,10 @@
         for j in range(C // COL):
             total[PROJ, pl.ds(j, BN, stride=C // COL), :] = grad[:, j * COL:(j + 1) * COL]
 
-    stores = []
-    def store(src, dst):
-        copy = pltpu.make_async_copy(src, dst, out_sem.at[len(stores)])
-        copy.start()
-        stores.append(copy)
-
     def block_output():
         for w in range(WIN):
             rows = pl.ds(w * BINS, BINS)
             out_v[w] = (x_v[w].astype(F32) + dot(mid[rows, :], p_v[...])).astype(BF16)
-        store(out_v, out_hbm)
 
     def outer_taps(ch):
         for w in range(WIN):
@@ -403,7 +396,6 @@
     straight(2)
     ring(1, 2)
     input_side(2)
-    store(dx_v, dx_hbm)
     along_z(0)
     along_z(PROJ)
     along_y(1)
@@ -426,7 +418,14 @@
             y_copy(rnd, k).wait_send()
         z_wait(rnd, False)
     finish(LAST)
-    for copy in stores:
+
+
+def write_out(*refs):
+    *refs, sem = refs
+    copies = [pltpu.make_async_copy(refs[i], refs[4 + i], sem.at[i]) for i in range(4)]
+    for copy in copies:
+        copy.start()
+    for copy in copies:
         copy.wait()
 
 
@@ -438,21 +437,17 @@
     halo = (CHUNKS, ROWS, COL)
     hbm = pl.BlockSpec(memory_space=pl.ANY)
     vmem = pl.BlockSpec(memory_space=pltpu.VMEM)
-    return pl.pallas_call(
+    results = pl.pallas_call(
         functools.partial(kernel, factor),
         out_shape=(
-            jax.ShapeDtypeStruct(inputs.shape, BF16),
-            jax.ShapeDtypeStruct(inputs.shape, BF16),
-            jax.ShapeDtypeStruct((CHUNKS * OWN, COL), F32),
-            jax.ShapeDtypeStruct((OWN, COL), F32),
+            vm(inputs.shape, BF16), vm(inputs.shape, BF16), vm((CHUNKS * OWN, COL), F32), vm((OWN, COL), F32),
         ),
         in_specs=[hbm] * 4,
-        out_specs=(hbm, hbm, vmem, vmem),
+        out_specs=(vmem,) * 4,
         scratch_shapes=[
             vm((WIN, BINS, C), BF16), vm((3, C, BN), BF16), vm((BN, C), BF16), vm((WIN, BINS, C), BF16),
             vm((ROWS, C), BF16), vm((C, ROWS), BF16), vm((ROWS, C), F32),
             vm((ROWS, BN), F32), vm((ROWS, BN), F32), vm((ROWS, BN), BF16), vm((ROWS, C), F32),
-            vm((WIN, BINS, C), BF16), vm((WIN, BINS, C), BF16),
             vm(halo, BF16), vm(halo, BF16), vm(halo, BF16), vm(halo, BF16),
             vm(halo, BF16), vm(halo, BF16), vm(halo, BF16),
             vm((ROUNDS, ALL, COL), F32),
@@ -463,17 +458,27 @@
             vm((ROUNDS, 3, UNIT + 8, COL), BF16), vm((ROUNDS, 3, UNIT + 8, COL), BF16),
             vm((ROUNDS, UNIT + 8, COL), F32),
             vm((ROUNDS, 8, 16, COL), BF16), vm((ROUNDS, 8, 16, COL), BF16),
-            dma((8,)), dma((2,)), dma((4,)),
+            dma((8,)), dma((4,)),
             dma((CHUNKS, WIN)), dma((CHUNKS, WIN)), dma((CHUNKS, WIN)), dma((CHUNKS, WIN)),
             dma((ROUNDS,)), dma((ROUNDS,)), dma((ROUNDS, 3)), dma((ROUNDS, 3)),
             dma((ROUNDS, 3)), dma((ROUNDS, 3)),
             dma((ROUNDS,)), dma((ROUNDS,)),
         ],
         compiler_params=pltpu.CompilerParams(
-            collective_id=0, has_side_effects=True, vmem_limit_bytes=56 * 1024 * 1024
+            collective_id=0, has_side_effects=True, vmem_limit_bytes=44 * 1024 * 1024
         ),
         name="block",
-    )(inputs, dilated_tap_weight, proj_weight, cotangent)
+    )(*[pltpu.with_memory_space_constraint(a, pltpu.HBM)
+        for a in (inputs, dilated_tap_weight, proj_weight, cotangent)])
+    results = [pltpu.with_memory_space_constraint(r, pltpu.VMEM) for r in results]
+    return pl.pallas_call(
+        write_out,
+        out_shape=tuple(jax.ShapeDtypeStruct(r.shape, r.dtype) for r in results),
+        in_specs=[vmem] * 4,
+        out_specs=(hbm,) * 4,
+        scratch_shapes=[dma((4,))],
+        name="write_out",
+    )(*results)
 
 
 def solution(mesh):

time: 70.1 us -> 66.2 us (0.944)
  local copies, waits for them, and re-layouts: 4.68 us -> 0 us
  Pallas kernels: 64.6 us -> 65.4 us
    unnamed x10 -> x0, local copies, waits for them, and re-layouts: 4.68 us -> none
    pallas_call x1 -> x2, Pallas kernels: 64.6 us -> 65.4 us  [the longest x1 64 us: local(): pl.pallas_call(functools.partial(kernel, factor), out_shape=(vm(inputs.sh...]
where the time goes in v3:
time: 66.2 us; the launch traced here: 66.1 us
  Pallas kernels  65.4 us (99%)
    pallas_call x1, Pallas kernels, local(): pl.pallas_call(functools.partial(kernel, factor), out_shape=(vm(inputs.sh...  64 us
    pallas_call x1, Pallas kernels, local(): pl.pallas_call(write_out, out_shape=tuple((jax.ShapeDtypeStruct(r.shape,...  1.44 us

profile of v3, /device:TPU:1, one launch (start us, length us, event | category | flops | bytes accessed | tf_op | source)
XLA Modules:
  0.0 66.1 jit_solution(9723793824995688311)
XLA Ops:
  0.6 64.0 %block.1 = (bf16[3,256,768]{2,1,0:T(8,128)(2,1)S(1)}, bf16[3,256,768]{2,1,0:T(8,128)(2,1)S(1)}, f32[27,128]{1,0:T(8,128)S(1)}, f32[9,128]{1,0:T(8,128)S(1)}) custom-call(bf16[3,256,768]{2,1,0:T(8,128)(2,1)} %x_hbm.1, bf16[3,768,384]{2,1,0:T(8,128)(2,1)} %w_hbm.1, bf16[384,768]{1,0:T(8,128)(2,1)} %p_hbm.1, bf16[3,256,768]{2,1,0:T(8,128)(2,1)} %g_hbm.1), custom_call_target="tpu_custom_call" | custom-call | tf_op jit(solution)/shard_map/block/pallas_call | solution.py:440
  64.6 1.4 %write_out.1 = (bf16[3,256,768]{2,1,0:T(8,128)(2,1)}, bf16[3,256,768]{2,1,0:T(8,128)(2,1)}, f32[27,128]{1,0:T(8,128)}, f32[9,128]{1,0:T(8,128)}) custom-call(bf16[3,256,768]{2,1,0:T(8,128)(2,1)S(1)} %get-tuple-element.8.refs_0_, bf16[3,256,768]{2,1,0:T(8,128)(2,1)S(1)} %get-tuple-element.9.refs_1_, f32[27,128]{1,0:T(8,128)S(1)} %get-tuple-element.10.refs_2_, ...), custom_call_target="tpu_custom_call" | custom-call | tf_op jit(solution)/shard_map/write_out/pallas_call | solution.py:474

commit v4 on v3

--- a/solution.py
+++ b/solution.py
@@ -24,6 +24,7 @@
 PROJ = CHUNKS
 ROUNDS = CHUNKS + 1
 LAST = CHUNKS - 1
+STRAIGHT = (LAST - 1, LAST)
 ALL = 2304
 UNIT = 72
 PART = 4 * UNIT
@@ -256,7 +257,7 @@
 
     def along_y(rnd):
         mine = both_cores(rnd, x)
-        if rnd == LAST:
+        if rnd in STRAIGHT:
             for k in (1, 3, 2):
                 x_copy(rnd, k).wait_recv()
             mine = mine + x_recv[rnd, 0].astype(F32) + x_recv[rnd, 1].astype(F32)
@@ -386,24 +387,22 @@
     stage_a(1)
     ring(PROJ, 1)
     input_side(1)
-    ring(1, 0)
+    straight(1)
     ring(PROJ, 2)
     outer_taps(2)
     stage_a(2)
-    ring(1, 1)
+    straight(2)
     along_y(0)
     along_y(PROJ)
-    straight(2)
-    ring(1, 2)
+    along_y(1)
     input_side(2)
     along_z(0)
+    along_y(2)
     along_z(PROJ)
-    along_y(1)
-    along_y(2)
     along_z(1)
+    along_z(2)
     finish(0)
     finish(PROJ)
-    along_z(2)
     finish(1)
 
     for i, (ref, to) in enumerate(((u_send, upper), (v_send, lower), (d_send, upper), (d_send, lower))):

time: 66.2 us -> 62.6 us (0.946)
  Pallas kernels: 65.4 us -> 61.9 us
    pallas_call x1, Pallas kernels: 64 us -> 60.4 us  [local(): pl.pallas_call(functools.partial(kernel, factor), out_shape=(vm(inputs.sh...]
where the time goes in v4:
time: 62.6 us; the launch traced here: 62.5 us
  Pallas kernels  61.9 us (99%)
  between operations  0.64 us (1%)
    pallas_call x1, Pallas kernels, local(): pl.pallas_call(functools.partial(kernel, factor), out_shape=(vm(inputs.sh...  60.4 us
    pallas_call x1, Pallas kernels, local(): pl.pallas_call(write_out, out_shape=tuple((jax.ShapeDtypeStruct(r.shape,...  1.44 us

profile of v4, /device:TPU:1, one launch (start us, length us, event | category | flops | bytes accessed | tf_op | source)
XLA Modules:
  0.0 62.5 jit_solution(3891122581312859159)
XLA Ops:
  0.6 60.4 %block.1 = (bf16[3,256,768]{2,1,0:T(8,128)(2,1)S(1)}, bf16[3,256,768]{2,1,0:T(8,128)(2,1)S(1)}, f32[27,128]{1,0:T(8,128)S(1)}, f32[9,128]{1,0:T(8,128)S(1)}) custom-call(bf16[3,256,768]{2,1,0:T(8,128)(2,1)} %x_hbm.1, bf16[3,768,384]{2,1,0:T(8,128)(2,1)} %w_hbm.1, bf16[384,768]{1,0:T(8,128)(2,1)} %p_hbm.1, bf16[3,256,768]{2,1,0:T(8,128)(2,1)} %g_hbm.1), custom_call_target="tpu_custom_call" | custom-call | tf_op jit(solution)/shard_map/block/pallas_call | solution.py:439
  61.1 1.4 %write_out.1 = (bf16[3,256,768]{2,1,0:T(8,128)(2,1)}, bf16[3,256,768]{2,1,0:T(8,128)(2,1)}, f32[27,128]{1,0:T(8,128)}, f32[9,128]{1,0:T(8,128)}) custom-call(bf16[3,256,768]{2,1,0:T(8,128)(2,1)S(1)} %get-tuple-element.8.refs_0_, bf16[3,256,768]{2,1,0:T(8,128)(2,1)S(1)} %get-tuple-element.9.refs_1_, f32[27,128]{1,0:T(8,128)S(1)} %get-tuple-element.10.refs_2_, ...), custom_call_target="tpu_custom_call" | custom-call | tf_op jit(solution)/shard_map/write_out/pallas_call | solution.py:473

commit v5 on v4

--- a/solution.py
+++ b/solution.py
@@ -24,7 +24,7 @@
 PROJ = CHUNKS
 ROUNDS = CHUNKS + 1
 LAST = CHUNKS - 1
-STRAIGHT = (LAST - 1, LAST)
+STRAIGHT = (LAST - 1,)
 ALL = 2304
 UNIT = 72
 PART = 4 * UNIT
@@ -53,8 +53,9 @@
     u_send, v_send, u_recv, v_recv, d_send, dup_recv, dlo_recv,
     total, pair_send, pair_recv, x_send, x_recv, acc,
     y_sum, y_send, y_recv, z_sum, z_send, z_recv,
+    p_acc, p_sum, p_send, p_recv,
     in_sem, ph_send_sem, u_sem, v_sem, dup_sem, dlo_sem,
-    pair_ssem, pair_rsem, x_ssem, x_rsem, y_ssem, y_rsem, z_ssem, z_rsem,
+    pair_ssem, pair_rsem, x_ssem, x_rsem, y_ssem, y_rsem, z_ssem, z_rsem, p_sem,
 ):
     zh = lax.axis_index("dp")
     s = lax.axis_index("seq")
@@ -93,6 +94,8 @@
     for k in (1, 2, 3):
         greet(device(zh, lax.rem(x + k, 4), zl, y, c))
         greet(device(zh, x, zl, lax.rem(y + k, 4), c))
+        for j in (1, 2, 3):
+            greet(device(zh, lax.rem(x + k, 4), zl, lax.rem(y + j, 4), c))
     for kz in range(4):
         for kl in range(2):
             peer = device(lax.rem(zh + kz, 4), x, lax.rem(zl + c + kl, 2), y, zl)
@@ -139,7 +142,7 @@
         for ch in range(CHUNKS):
             u_send[ch, pl.ds(w * BINS, BINS), :] = u[:, ch * COL:(ch + 1) * COL]
         if w == 0:
-            pl.semaphore_wait(barrier, 2 + 1 + 3 + 3 + 7 + off)
+            pl.semaphore_wait(barrier, 2 + 1 + 15 + 7 + off)
         send_halo(u_send, u_recv, u_sem, 0, 0, w, upper)
         if w == 0:
             loads["w2"].wait()
@@ -272,6 +275,32 @@
             y_send[rnd, k - 1] = y_sum[rnd, lax.rem(y + k, 4)].astype(BF16)
             y_copy(rnd, k).start()
 
+    def plane_copy(kx, ky):
+        return pltpu.make_async_remote_copy(
+            src_ref=p_send.at[kx * 4 + ky], dst_ref=p_recv.at[kx * 4 + ky],
+            send_sem=p_sem.at[0], recv_sem=p_sem.at[1],
+            device_id=device(zh, lax.rem(x + kx, 4), zl, lax.rem(y + ky, 4), c), device_id_type=MESH,
+        )
+
+    def plane(rnd):
+        pair_copy(rnd).wait_recv()
+        for kx in (2, 1, 3, 0):
+            p_acc[kx] = both_cores(rnd, lax.rem(x + kx, 4))
+            for ya in range(4):
+                for za in range(4):
+                    p_sum[kx, ya, pl.ds(za * LINE, LINE), :] = p_acc[kx, pl.ds(za * UNIT + ya * LINE, LINE), :]
+                p_sum[kx, ya, pl.ds(UNIT, 8), :] = jnp.zeros((8, COL), F32)
+            for ky in (2, 1, 3, 0):
+                if kx or ky:
+                    p_send[kx * 4 + ky] = p_sum[kx, lax.rem(y + ky, 4)].astype(BF16)
+                    plane_copy(kx, ky).start()
+
+    def plane_wait():
+        return pltpu.make_async_remote_copy(
+            src_ref=p_send.at[pl.ds(1, 15)], dst_ref=p_recv.at[pl.ds(1, 15)],
+            send_sem=p_sem.at[0], recv_sem=p_sem.at[1], device_id=sibling, device_id_type=MESH,
+        )
+
     def z_copy(rnd, kz, kc):
         za = lax.rem(zh + kz, 4)
         ca = lax.rem(c + kc, 2)
@@ -282,12 +311,16 @@
         )
 
     def along_z(rnd):
-        for k in (1, 3, 2):
-            y_copy(rnd, k).wait_recv()
-        z_sum[rnd] = (
-            y_sum[rnd, y] + y_recv[rnd, 0].astype(F32)
-            + y_recv[rnd, 1].astype(F32) + y_recv[rnd, 2].astype(F32)
-        )
+        if rnd == LAST:
+            plane_wait().wait_recv()
+            z_sum[rnd] = p_sum[0, y] + jnp.sum(p_recv[pl.ds(1, 15)].astype(F32), axis=0)
+        else:
+            for k in (1, 3, 2):
+                y_copy(rnd, k).wait_recv()
+            z_sum[rnd] = (
+                y_sum[rnd, y] + y_recv[rnd, 0].astype(F32)
+                + y_recv[rnd, 1].astype(F32) + y_recv[rnd, 2].astype(F32)
+            )
         for b in range(8):
             z_send[rnd, b] = z_sum[rnd, pl.ds(OWN * b, 16), :].astype(BF16)
         for kz in (2, 1, 3, 0):
@@ -342,13 +375,25 @@
             out_v[w] = (x_v[w].astype(F32) + dot(mid[rows, :], p_v[...])).astype(BF16)
 
     def outer_taps(ch):
+        first = WIN - 1
         for w in range(WIN):
             wait_halo(dup_recv, dup_sem, ch, w)
             wait_halo(dlo_recv, dlo_sem, ch, w)
             clear_if(s < 2, dlo_recv, ch, w)
             clear_if(s >= 62, dup_recv, ch, w)
-        total[ch, pl.ds(0, C), :] = dot(act_t[...], dup_recv[ch])
-        total[ch, pl.ds(2 * C, C), :] = dot(act_t[...], dlo_recv[ch])
+            if w < first - 1:
+                continue
+            rows = pl.ds(0, first * BINS) if w == first - 1 else pl.ds(w * BINS, BINS)
+            both = jnp.concatenate([dup_recv[ch, rows, :], dlo_recv[ch, rows, :]], axis=1)
+            for m in range(WIN):
+                term = dot(act_t[pl.ds(m * BINS, BINS), rows], both)
+                low, high = pl.ds(m * BINS, BINS), pl.ds(2 * C + m * BINS, BINS)
+                if w == first - 1:
+                    total[ch, low, :] = term[:, :COL]
+                    total[ch, high, :] = term[:, COL:]
+                else:
+                    total[ch, low, :] = total[ch, low, :] + term[:, :COL]
+                    total[ch, high, :] = total[ch, high, :] + term[:, COL:]
 
     def input_side(ch):
         cols = pl.ds(ch * COL, COL)
@@ -391,13 +436,12 @@
     ring(PROJ, 2)
     outer_taps(2)
     stage_a(2)
-    straight(2)
     along_y(0)
+    plane(2)
     along_y(PROJ)
     along_y(1)
     input_side(2)
     along_z(0)
-    along_y(2)
     along_z(PROJ)
     along_z(1)
     along_z(2)
@@ -412,9 +456,12 @@
         ).wait_send()
     for rnd in range(ROUNDS):
         pair_copy(rnd).wait_send()
-        for k in (1, 2, 3):
-            x_copy(rnd, k).wait_send()
-            y_copy(rnd, k).wait_send()
+        if rnd == LAST:
+            plane_wait().wait_send()
+        else:
+            for k in (1, 2, 3):
+                x_copy(rnd, k).wait_send()
+                y_copy(rnd, k).wait_send()
         z_wait(rnd, False)
     finish(LAST)
 
@@ -457,11 +504,13 @@
             vm((ROUNDS, 3, UNIT + 8, COL), BF16), vm((ROUNDS, 3, UNIT + 8, COL), BF16),
             vm((ROUNDS, UNIT + 8, COL), F32),
             vm((ROUNDS, 8, 16, COL), BF16), vm((ROUNDS, 8, 16, COL), BF16),
+            vm((4, PART, COL), F32), vm((4, 4, UNIT + 8, COL), F32),
+            vm((16, UNIT + 8, COL), BF16), vm((16, UNIT + 8, COL), BF16),
             dma((8,)), dma((4,)),
             dma((CHUNKS, WIN)), dma((CHUNKS, WIN)), dma((CHUNKS, WIN)), dma((CHUNKS, WIN)),
             dma((ROUNDS,)), dma((ROUNDS,)), dma((ROUNDS, 3)), dma((ROUNDS, 3)),
             dma((ROUNDS, 3)), dma((ROUNDS, 3)),
-            dma((ROUNDS,)), dma((ROUNDS,)),
+            dma((ROUNDS,)), dma((ROUNDS,)), dma((2,)),
         ],
         compiler_params=pltpu.CompilerParams(
             collective_id=0, has_side_effects=True, vmem_limit_bytes=44 * 1024 * 1024

time: 62.6 us -> 60.6 us (0.968)
  Pallas kernels: 61.9 us -> 59.9 us
    pallas_call x1, Pallas kernels: 60.4 us -> 58.5 us  [local(): pl.pallas_call(functools.partial(kernel, factor), out_shape=(vm(inputs.sh...]
where the time goes in v5:
time: 60.6 us; the launch traced here: 60.5 us
  Pallas kernels  59.9 us (99%)
  between operations  0.64 us (1%)
    pallas_call x1, Pallas kernels, local(): pl.pallas_call(functools.partial(kernel, factor), out_shape=(vm(inputs.sh...  58.5 us
    pallas_call x1, Pallas kernels, local(): pl.pallas_call(write_out, out_shape=tuple((jax.ShapeDtypeStruct(r.shape,...  1.44 us

profile of v5, /device:TPU:1, one launch (start us, length us, event | category | flops | bytes accessed | tf_op | source)
XLA Modules:
  0.0 60.5 jit_solution(6253412718835100285)
XLA Ops:
  0.6 58.5 %block.1 = (bf16[3,256,768]{2,1,0:T(8,128)(2,1)S(1)}, bf16[3,256,768]{2,1,0:T(8,128)(2,1)S(1)}, f32[27,128]{1,0:T(8,128)S(1)}, f32[9,128]{1,0:T(8,128)S(1)}) custom-call(bf16[3,256,768]{2,1,0:T(8,128)(2,1)} %x_hbm.1, bf16[3,768,384]{2,1,0:T(8,128)(2,1)} %w_hbm.1, bf16[384,768]{1,0:T(8,128)(2,1)} %p_hbm.1, bf16[3,256,768]{2,1,0:T(8,128)(2,1)} %g_hbm.1), custom_call_target="tpu_custom_call" | custom-call | tf_op jit(solution)/shard_map/block/pallas_call | solution.py:486
  59.1 1.4 %write_out.1 = (bf16[3,256,768]{2,1,0:T(8,128)(2,1)}, bf16[3,256,768]{2,1,0:T(8,128)(2,1)}, f32[27,128]{1,0:T(8,128)}, f32[9,128]{1,0:T(8,128)}) custom-call(bf16[3,256,768]{2,1,0:T(8,128)(2,1)S(1)} %get-tuple-element.8.refs_0_, bf16[3,256,768]{2,1,0:T(8,128)(2,1)S(1)} %get-tuple-element.9.refs_1_, f32[27,128]{1,0:T(8,128)S(1)} %get-tuple-element.10.refs_2_, ...), custom_call_target="tpu_custom_call" | custom-call | tf_op jit(solution)/shard_map/write_out/pallas_call | solution.py:522

commit v6 on v5

--- a/solution.py
+++ b/solution.py
@@ -24,7 +24,7 @@
 PROJ = CHUNKS
 ROUNDS = CHUNKS + 1
 LAST = CHUNKS - 1
-STRAIGHT = (LAST - 1,)
+STRAIGHT = (LAST - 1, PROJ)
 ALL = 2304
 UNIT = 72
 PART = 4 * UNIT
@@ -202,17 +202,24 @@
     def part(rnd, x_, zl_):
         return jnp.concatenate([unit(rnd, k, x_, zl_) for k in range(4)], axis=0)
 
-    def pair_copy(rnd):
-        return pltpu.make_async_remote_copy(
-            src_ref=pair_send.at[rnd], dst_ref=pair_recv.at[rnd],
-            send_sem=pair_ssem.at[rnd], recv_sem=pair_rsem.at[rnd],
+    def part_rows(k):
+        return pl.ds(pl.multiple_of(lax.rem(x + k, 4) * PART, 16), PART)
+
+    def pair_copy(rnd, k):
+        return pltpu.make_async_remote_copy(
+            src_ref=pair_send.at[rnd, part_rows(k)], dst_ref=pair_recv.at[rnd, part_rows(k)],
+            send_sem=pair_ssem.at[rnd, k], recv_sem=pair_rsem.at[rnd, k],
             device_id=sibling, device_id_type=MESH,
         )
 
     def stage_a(rnd):
-        for xa in range(4):
-            pair_send[rnd, pl.ds(xa * PART, PART), :] = part(rnd, xa, 1 - c).astype(BF16)
-        pair_copy(rnd).start()
+        for k in (2, 1, 3, 0):
+            pair_send[rnd, part_rows(k), :] = part(rnd, lax.rem(x + k, 4), 1 - c).astype(BF16)
+            pair_copy(rnd, k).start()
+
+    def pair_wait(rnd):
+        for k in range(4):
+            pair_copy(rnd, k).wait_recv()
 
     def x_copy(rnd, k):
         return pltpu.make_async_remote_copy(
@@ -236,7 +243,7 @@
 
     def ring(rnd, t):
         if t == 0:
-            pair_copy(rnd).wait_recv()
+            pair_wait(rnd)
             part_sum = both_cores(rnd, lax.rem(x + 4 - step, 4))
         else:
             ring_copy(rnd, t - 1).wait_recv()
@@ -246,7 +253,7 @@
         ring_copy(rnd, t).start()
 
     def straight(rnd):
-        pair_copy(rnd).wait_recv()
+        pair_wait(rnd)
         for k in (2, 1, 3):
             x_send[rnd, k - 1] = both_cores(rnd, lax.rem(x + k, 4)).astype(BF16)
             x_copy(rnd, k).start()
@@ -283,8 +290,8 @@
         )
 
     def plane(rnd):
-        pair_copy(rnd).wait_recv()
         for kx in (2, 1, 3, 0):
+            pair_copy(rnd, kx).wait_recv()
             p_acc[kx] = both_cores(rnd, lax.rem(x + kx, 4))
             for ya in range(4):
                 for za in range(4):
@@ -426,14 +433,12 @@
     projection()
     stage_a(PROJ)
     block_output()
-    ring(PROJ, 0)
+    straight(PROJ)
     ring(0, 2)
     outer_taps(1)
     stage_a(1)
-    ring(PROJ, 1)
     input_side(1)
     straight(1)
-    ring(PROJ, 2)
     outer_taps(2)
     stage_a(2)
     along_y(0)
@@ -455,7 +460,8 @@
             device_id=to, device_id_type=MESH,
         ).wait_send()
     for rnd in range(ROUNDS):
-        pair_copy(rnd).wait_send()
+        for k in range(4):
+            pair_copy(rnd, k).wait_send()
         if rnd == LAST:
             plane_wait().wait_send()
         else:
@@ -508,7 +514,7 @@
             vm((16, UNIT + 8, COL), BF16), vm((16, UNIT + 8, COL), BF16),
             dma((8,)), dma((4,)),
             dma((CHUNKS, WIN)), dma((CHUNKS, WIN)), dma((CHUNKS, WIN)), dma((CHUNKS, WIN)),
-            dma((ROUNDS,)), dma((ROUNDS,)), dma((ROUNDS, 3)), dma((ROUNDS, 3)),
+            dma((ROUNDS, 4)), dma((ROUNDS, 4)), dma((ROUNDS, 3)), dma((ROUNDS, 3)),
             dma((ROUNDS, 3)), dma((ROUNDS, 3)),
             dma((ROUNDS,)), dma((ROUNDS,)), dma((2,)),
         ],

time: 60.6 us -> 58 us (0.957)
  Pallas kernels: 59.9 us -> 57.3 us
    pallas_call x1, Pallas kernels: 58.5 us -> 55.9 us  [local(): pl.pallas_call(functools.partial(kernel, factor), out_shape=(vm(inputs.sh...]
where the time goes in v6:
time: 58 us; the launch traced here: 57.9 us
  Pallas kernels  57.3 us (99%)
  between operations  0.64 us (1%)
    pallas_call x1, Pallas kernels, local(): pl.pallas_call(functools.partial(kernel, factor), out_shape=(vm(inputs.sh...  55.9 us
    pallas_call x1, Pallas kernels, local(): pl.pallas_call(write_out, out_shape=tuple((jax.ShapeDtypeStruct(r.shape,...  1.44 us

profile of v6, /device:TPU:1, one launch (start us, length us, event | category | flops | bytes accessed | tf_op | source)
XLA Modules:
  0.0 57.9 jit_solution(3729214285288596970)
XLA Ops:
  0.6 55.9 %block.1 = (bf16[3,256,768]{2,1,0:T(8,128)(2,1)S(1)}, bf16[3,256,768]{2,1,0:T(8,128)(2,1)S(1)}, f32[27,128]{1,0:T(8,128)S(1)}, f32[9,128]{1,0:T(8,128)S(1)}) custom-call(bf16[3,256,768]{2,1,0:T(8,128)(2,1)} %x_hbm.1, bf16[3,768,384]{2,1,0:T(8,128)(2,1)} %w_hbm.1, bf16[384,768]{1,0:T(8,128)(2,1)} %p_hbm.1, bf16[3,256,768]{2,1,0:T(8,128)(2,1)} %g_hbm.1), custom_call_target="tpu_custom_call" | custom-call | tf_op jit(solution)/shard_map/block/pallas_call | solution.py:492
  56.5 1.4 %write_out.1 = (bf16[3,256,768]{2,1,0:T(8,128)(2,1)}, bf16[3,256,768]{2,1,0:T(8,128)(2,1)}, f32[27,128]{1,0:T(8,128)}, f32[9,128]{1,0:T(8,128)}) custom-call(bf16[3,256,768]{2,1,0:T(8,128)(2,1)S(1)} %get-tuple-element.8.refs_0_, bf16[3,256,768]{2,1,0:T(8,128)(2,1)S(1)} %get-tuple-element.9.refs_1_, f32[27,128]{1,0:T(8,128)S(1)} %get-tuple-element.10.refs_2_, ...), custom_call_target="tpu_custom_call" | custom-call | tf_op jit(solution)/shard_map/write_out/pallas_call | solution.py:528

commit v7 on v6

--- a/solution.py
+++ b/solution.py
@@ -442,8 +442,8 @@
     outer_taps(2)
     stage_a(2)
     along_y(0)
+    along_y(PROJ)
     plane(2)
-    along_y(PROJ)
     along_y(1)
     input_side(2)
     along_z(0)

time: 58 us -> 58 us (level)
  no operation moved by 1% of the time
where the time goes in v7:
time: 58 us; the launch traced here: 57.9 us
  Pallas kernels  57.3 us (99%)
  between operations  0.64 us (1%)
    pallas_call x1, Pallas kernels, local(): pl.pallas_call(functools.partial(kernel, factor), out_shape=(vm(inputs.sh...  55.9 us
    pallas_call x1, Pallas kernels, local(): pl.pallas_call(write_out, out_shape=tuple((jax.ShapeDtypeStruct(r.shape,...  1.44 us

profile of v7, /device:TPU:1, one launch (start us, length us, event | category | flops | bytes accessed | tf_op | source)
XLA Modules:
  0.0 57.9 jit_solution(6561260425409694482)
XLA Ops:
  0.6 55.9 %block.1 = (bf16[3,256,768]{2,1,0:T(8,128)(2,1)S(1)}, bf16[3,256,768]{2,1,0:T(8,128)(2,1)S(1)}, f32[27,128]{1,0:T(8,128)S(1)}, f32[9,128]{1,0:T(8,128)S(1)}) custom-call(bf16[3,256,768]{2,1,0:T(8,128)(2,1)} %x_hbm.1, bf16[3,768,384]{2,1,0:T(8,128)(2,1)} %w_hbm.1, bf16[384,768]{1,0:T(8,128)(2,1)} %p_hbm.1, bf16[3,256,768]{2,1,0:T(8,128)(2,1)} %g_hbm.1), custom_call_target="tpu_custom_call" | custom-call | tf_op jit(solution)/shard_map/block/pallas_call | solution.py:492
  56.5 1.4 %write_out.1 = (bf16[3,256,768]{2,1,0:T(8,128)(2,1)}, bf16[3,256,768]{2,1,0:T(8,128)(2,1)}, f32[27,128]{1,0:T(8,128)}, f32[9,128]{1,0:T(8,128)}) custom-call(bf16[3,256,768]{2,1,0:T(8,128)(2,1)S(1)} %get-tuple-element.8.refs_0_, bf16[3,256,768]{2,1,0:T(8,128)(2,1)S(1)} %get-tuple-element.9.refs_1_, f32[27,128]{1,0:T(8,128)S(1)} %get-tuple-element.10.refs_2_, ...), custom_call_target="tpu_custom_call" | custom-call | tf_op jit(solution)/shard_map/write_out/pallas_call | solution.py:528
